TPU v7x, 32 devices: a whole 2x2x4 slice. The times are simulated.
32 devices in a mesh: dp: 8 (over z, x), mp: 4 (over y, core).
Axes of the slice: x: 2, y: 2, z: 4, core: 2. Of those that a mesh axis runs over, the one named last changes fastest.
Arguments:
- tokens: bfloat16 [16384, 768], P('dp'), may hold values from -6 to 6
- lengths: int32 [32], P('dp'), may hold values from 60 to 512, as said below
- query_weight: bfloat16 [768, 768], P(None, 'mp'), may hold values from -0.21875 to 0.21875
- query_bias: bfloat16 [768], P('mp'), may hold values from -3 to 3
- key_weight: bfloat16 [768, 768], P(None, 'mp'), may hold values from -0.21875 to 0.21875
- value_weight: bfloat16 [768, 768], P(None, 'mp'), may hold values from -0.21875 to 0.21875
- value_bias: bfloat16 [768], P('mp'), may hold values from -3 to 3
- out_weight: bfloat16 [768, 768], P('mp'), may hold values from -0.875 to 0.875
- out_bias: bfloat16 [768], replicated, may hold values from -2 to 2
- attn_gain: bfloat16 [768], replicated, may hold values from 0.5 to 1.5
- attn_shift: bfloat16 [768], replicated, may hold values from -2 to 2
- up_weight: bfloat16 [768, 3072], P(None, 'mp'), may hold values from -0.21875 to 0.21875
- up_bias: bfloat16 [3072], P('mp'), may hold values from -3 to 3
- down_weight: bfloat16 [3072, 768], P('mp'), may hold values from -0.109375 to 0.109375
- down_bias: bfloat16 [768], replicated, may hold values from -2 to 2
- ffn_gain: bfloat16 [768], replicated, may hold values from 0.5 to 1.5
- ffn_shift: bfloat16 [768], replicated, may hold values from -2 to 2
- cotangent: bfloat16 [16384, 768], P('dp'), may hold values from -6 to 6
Outputs:
- layer_out: bfloat16 [16384, 768], P('dp')
- tokens_grad: bfloat16 [16384, 768], P('dp')
- query_weight_grad: float32 [768, 768], P(None, 'mp')
- query_bias_grad: float32 [768], P('mp')
- key_weight_grad: float32 [768, 768], P(None, 'mp')
- value_weight_grad: float32 [768, 768], P(None, 'mp')
- value_bias_grad: float32 [768], P('mp')
- out_weight_grad: float32 [768, 768], P('mp')
- out_bias_grad: float32 [768], replicated
- attn_gain_grad: float32 [768], replicated
- attn_shift_grad: float32 [768], replicated
- up_weight_grad: float32 [768, 3072], P(None, 'mp')
- up_bias_grad: float32 [3072], P('mp')
- down_weight_grad: float32 [3072, 768], P('mp')
- down_bias_grad: float32 [768], replicated
- ffn_gain_grad: float32 [768], replicated
- ffn_shift_grad: float32 [768], replicated
Inputs may be any that keep to these rules, and one draw needn't show every extreme that they name: `lengths`: in every draw some table has all 512 tokens live and some has the fewest allowed.
All inputs are finite; a program needn't handle non-finite values.
Results may differ from a plain program's by a relative error of at most 0.022.
Values may be sent and summed in bfloat16 or wider, within the bound.
A program may use at most 128 MiB of HBM per device.

v0:
```python
import jax
import jax.numpy as jnp
from jax import lax
from jax.sharding import PartitionSpec as P

HD = 64


EPS = 1e-06


def outer_rows(left, right):
    return lax.dot_general(
        left, right, (((0,), (0,)), ((), ())), preferred_element_type=jnp.float32
    )


def inner_cols(left, right):
    return lax.dot_general(
        left, right, (((1,), (1,)), ((), ())), preferred_element_type=jnp.float32
    )


def normalize_parts(mixed_rows, gain_row, shift_row):
    center = mixed_rows - jnp.mean(mixed_rows, axis=-1, keepdims=True)
    inv_std = lax.rsqrt(jnp.mean(center * center, axis=-1, keepdims=True) + EPS)
    normed = center * inv_std
    return (normed * gain_row + shift_row, normed, inv_std)


def normalize_back(upstream, normed, inv_std, gain_row):
    scaled = upstream * gain_row
    inner_part = (
        scaled
        - jnp.mean(scaled, axis=-1, keepdims=True)
        - normed * jnp.mean(scaled * normed, axis=-1, keepdims=True)
    )
    return (inner_part * inv_std, jnp.sum(upstream * normed, axis=0), jnp.sum(upstream, axis=0))


def split_heads(row_block):
    return row_block.reshape(row_block.shape[0], -1, HD).transpose(1, 0, 2)


def join_heads(head_block):
    return head_block.transpose(1, 0, 2).reshape(head_block.shape[1], -1)


def masked_scores(query_heads, key_heads, length):
    scores = jnp.einsum(
        "hqd,hkd->hqk", query_heads, key_heads, preferred_element_type=jnp.float32
    ) * HD ** (-0.5)
    live_keys = lax.iota(jnp.int32, key_heads.shape[1]) < length
    return jnp.where(live_keys[None, None, :], scores, -1e30)


def attend_forward(pieces):
    queries, key_rows, value_rows, length = pieces
    scores = masked_scores(split_heads(queries), split_heads(key_rows), length)
    row_top = jnp.max(scores, axis=-1, keepdims=True)
    exponent = jnp.exp(scores - row_top)
    row_sum = jnp.sum(exponent, axis=-1, keepdims=True)
    prob_low = (exponent / row_sum).astype(jnp.bfloat16)
    attended = jnp.einsum(
        "hqk,hkd->hqd", prob_low, split_heads(value_rows), preferred_element_type=jnp.float32
    )
    return (join_heads(attended).astype(jnp.bfloat16), (row_top + jnp.log(row_sum))[..., 0])


def attend_back(pieces):
    queries, key_rows, value_rows, length, log_total, upstream = pieces
    query_heads = split_heads(queries)
    key_heads = split_heads(key_rows)
    value_heads = split_heads(value_rows)
    scores = masked_scores(query_heads, key_heads, length)
    prob_rows = jnp.exp(scores - log_total[..., None])
    prob_low = prob_rows.astype(jnp.bfloat16)
    grad_heads = split_heads(upstream)
    grad_values = jnp.einsum(
        "hqk,hqd->hkd", prob_low, grad_heads, preferred_element_type=jnp.float32
    )
    grad_probs = jnp.einsum(
        "hqd,hkd->hqk", grad_heads, value_heads, preferred_element_type=jnp.float32
    )
    centered = grad_probs - jnp.sum(grad_probs * prob_rows, axis=-1, keepdims=True)
    grad_scores = (prob_rows * centered).astype(jnp.bfloat16)
    grad_queries = jnp.einsum(
        "hqk,hkd->hqd", grad_scores, key_heads, preferred_element_type=jnp.float32
    ) * HD ** (-0.5)
    grad_keys = jnp.einsum(
        "hqk,hqd->hkd", grad_scores, query_heads, preferred_element_type=jnp.float32
    ) * HD ** (-0.5)
    return (
        join_heads(grad_queries).astype(jnp.bfloat16),
        join_heads(grad_keys).astype(jnp.bfloat16),
        join_heads(grad_values).astype(jnp.bfloat16),
    )


def shards(
    tokens,
    lengths,
    query_weight,
    query_bias,
    key_weight,
    value_weight,
    value_bias,
    out_weight,
    out_bias,
    attn_gain,
    attn_shift,
    up_weight,
    up_bias,
    down_weight,
    down_bias,
    ffn_gain,
    ffn_shift,
    cotangent,
):
    table_count = lengths.shape[0]
    row_total = tokens.shape[0]
    seq_len = row_total // table_count
    head_width = query_weight.shape[1]

    def by_table(row_block):
        return row_block.reshape(table_count, seq_len, head_width)

    queries = (
        jnp.dot(tokens, query_weight, preferred_element_type=jnp.float32)
        + query_bias.astype(jnp.float32)
    ).astype(jnp.bfloat16)
    key_rows = jnp.dot(tokens, key_weight, preferred_element_type=jnp.float32).astype(jnp.bfloat16)
    value_rows = (
        jnp.dot(tokens, value_weight, preferred_element_type=jnp.float32)
        + value_bias.astype(jnp.float32)
    ).astype(jnp.bfloat16)
    attended, log_total = lax.map(
        attend_forward, (by_table(queries), by_table(key_rows), by_table(value_rows), lengths)
    )
    attended = attended.reshape(row_total, head_width)
    attention = lax.psum(
        jnp.dot(attended, out_weight, preferred_element_type=jnp.float32).astype(jnp.bfloat16), "mp"
    ).astype(jnp.float32)
    mixed_rows = tokens.astype(jnp.float32) + attention + out_bias.astype(jnp.float32)
    first_norm, first_normed, first_inv = normalize_parts(
        mixed_rows, attn_gain.astype(jnp.float32), attn_shift.astype(jnp.float32)
    )
    first_low = first_norm.astype(jnp.bfloat16)
    hidden = jnp.dot(first_low, up_weight, preferred_element_type=jnp.float32) + up_bias.astype(
        jnp.float32
    )
    activated = jax.nn.gelu(hidden, approximate=False).astype(jnp.bfloat16)
    ffn_total = lax.psum(
        jnp.dot(activated, down_weight, preferred_element_type=jnp.float32).astype(jnp.bfloat16),
        "mp",
    ).astype(jnp.float32)
    second_in = first_norm + ffn_total + down_bias.astype(jnp.float32)
    layer_out, second_normed, second_inv = normalize_parts(
        second_in, ffn_gain.astype(jnp.float32), ffn_shift.astype(jnp.float32)
    )
    grad_second, ffn_gain_grad, ffn_shift_grad = normalize_back(
        cotangent.astype(jnp.float32), second_normed, second_inv, ffn_gain.astype(jnp.float32)
    )
    down_bias_grad = jnp.sum(grad_second, axis=0)
    second_low = grad_second.astype(jnp.bfloat16)
    down_weight_grad = outer_rows(activated, second_low)
    grad_activated = inner_cols(second_low, down_weight)
    gelu_value, gelu_pull = jax.vjp(lambda inputs: jax.nn.gelu(inputs, approximate=False), hidden)
    grad_hidden = gelu_pull(grad_activated)[0].astype(jnp.bfloat16)
    up_bias_grad = jnp.sum(grad_hidden.astype(jnp.float32), axis=0)
    up_weight_grad = outer_rows(first_low, grad_hidden)
    grad_first = grad_second + lax.psum(
        inner_cols(grad_hidden, up_weight).astype(jnp.bfloat16), "mp"
    ).astype(jnp.float32)
    grad_mixed, attn_gain_grad, attn_shift_grad = normalize_back(
        grad_first, first_normed, first_inv, attn_gain.astype(jnp.float32)
    )
    out_bias_grad = jnp.sum(grad_mixed, axis=0)
    mixed_low = grad_mixed.astype(jnp.bfloat16)
    out_weight_grad = outer_rows(attended, mixed_low)
    grad_attended = inner_cols(mixed_low, out_weight).astype(jnp.bfloat16)
    grad_queries, grad_keys, grad_values = lax.map(
        attend_back,
        (
            by_table(queries),
            by_table(key_rows),
            by_table(value_rows),
            lengths,
            log_total,
            by_table(grad_attended),
        ),
    )
    grad_queries = grad_queries.reshape(row_total, head_width)
    grad_keys = grad_keys.reshape(row_total, head_width)
    grad_values = grad_values.reshape(row_total, head_width)
    query_bias_grad = jnp.sum(grad_queries.astype(jnp.float32), axis=0)
    value_bias_grad = jnp.sum(grad_values.astype(jnp.float32), axis=0)
    query_weight_grad = outer_rows(tokens, grad_queries)
    key_weight_grad = outer_rows(tokens, grad_keys)
    value_weight_grad = outer_rows(tokens, grad_values)
    back_tokens = (
        inner_cols(grad_queries, query_weight)
        + inner_cols(grad_keys, key_weight)
        + inner_cols(grad_values, value_weight)
    )
    tokens_grad = (
        grad_mixed + lax.psum(back_tokens.astype(jnp.bfloat16), "mp").astype(jnp.float32)
    ).astype(jnp.bfloat16)
    summed = lax.psum(
        (
            query_weight_grad,
            query_bias_grad,
            key_weight_grad,
            value_weight_grad,
            value_bias_grad,
            out_weight_grad,
            out_bias_grad,
            attn_gain_grad,
            attn_shift_grad,
            up_weight_grad,
            up_bias_grad,
            down_weight_grad,
            down_bias_grad,
            ffn_gain_grad,
            ffn_shift_grad,
        ),
        "dp",
    )
    return (
        layer_out.astype(jnp.bfloat16),
        tokens_grad,
        summed[0],
        summed[1],
        summed[2],
        summed[3],
        summed[4],
        summed[5],
        summed[6],
        summed[7],
        summed[8],
        summed[9],
        summed[10],
        summed[11],
        summed[12],
        summed[13],
        summed[14],
    )


def solution(mesh):
    in_specs = (
        P("dp", None),
        P("dp"),
        P(None, "mp"),
        P("mp"),
        P(None, "mp"),
        P(None, "mp"),
        P("mp"),
        P("mp", None),
        P(),
        P(),
        P(),
        P(None, "mp"),
        P("mp"),
        P("mp", None),
        P(),
        P(),
        P(),
        P("dp", None),
    )
    out_specs = (
        P("dp", None),
        P("dp", None),
        P(None, "mp"),
        P("mp"),
        P(None, "mp"),
        P(None, "mp"),
        P("mp"),
        P("mp", None),
        P(),
        P(),
        P(),
        P(None, "mp"),
        P("mp"),
        P("mp", None),
        P(),
        P(),
        P(),
    )
    return jax.shard_map(shards, mesh=mesh, in_specs=in_specs, out_specs=out_specs, check_vma=False)
```

profile of v0, /device:TPU:0, one launch (start us, length us, event | category | flops | bytes accessed | tf_op | source)
XLA Modules:
  0.0 710.9 jit_solution(17338435150115336313)
XLA Ops:
  9.0 4.0 convolution_convert_fusion.4
  14.3 3.1 fusion.29
  18.5 20.2 %while.26 = (s32[]{:T(128)}, bf16[4,512,192]{1,2,0:T(8,128)(2,1)}, f32[4,3,512]{2,1,0:T(4,128)}, s32[4]{0:T(128)S(1)}, bf16[4,512,192]{1,2,0:T(8,128)(2,1)S(1)},...) while((s32[]{:T(128)}, bf16[4,512,192]{1,2,0:T(8,128)(2,1)}, ...), condition=%wide.region_3.4_spmd, body=%wide.region_0.3_spmd.sunk | while | flops 210861056 | bytes 11850861 | solution.py:137
  41.0 3.7 convolution_convert_fusion.2
  47.3 68.6 %all-reduce.8.cloned.1.call-done = bf16[2048,768]{1,0:T(8,128)(2,1)} async-done(((bf16[2048,768]{1,0:T(8,128)(2,1)}), bf16[2048,768]{1,0:T(8,128)(2,1)}) %all-reduce.8.cloned.1.call-update) | async-done | bytes 3145744 | tf_op jit(solution)/shard_map/psum | solution.py:141
  115.9 4.1 fusion.27
  122.5 18.6 %multiply_convert_fusion.1 = (bf16[2048,768]{1,0:T(8,128)(2,1)S(1)}, f32[2048,768]{1,0:T(8,128)}, f32[2048,768]{1,0:T(8,128)}) fusion(f32[768]{0:T(1024)S(1)} %copy-done.32, bf16[768,768]{1,0:T(8,128)(2,1)S(1)} %copy-done, f32[768]{0:T(1024)S(1)} %copy-done.29, f32[768]{0:T(1024)S(1)} %convert_element_type.185, f32[2048]{0:T(1024)S(1)} %add_rsqrt_fusion.1, ...), kind=kOutput, calls=%fused_computation.57 | convolution fusion | flops 2533883904 | bytes 23228416 | tf_op jit(solution)/shard_map/dot_general | solution.py:149
  142.7 3.9 convolution_convert_fusion.1
  150.7 64.6 %all-reduce.10.cloned.1.call-done = bf16[2048,768]{1,0:T(8,128)(2,1)} async-done(((bf16[2048,768]{1,0:T(8,128)(2,1)}), bf16[2048,768]{1,0:T(8,128)(2,1)}) %all-reduce.10.cloned.1.call-update) | async-done | bytes 3145744 | tf_op jit(solution)/shard_map/psum | solution.py:153
  215.4 5.4 fusion.45
  222.7 3.6 fusion.20
  226.4 4.0 fusion.17
  230.3 9.5 %convert_reduce_fusion.1 = (f32[768]{0:T(1024)}, bf16[2048,768]{1,0:T(8,128)(2,1)S(1)}) fusion(f32[2048,768]{1,0:T(8,128)S(1)} %bitcast.201, bf16[768,768]{1,0:T(8,128)(2,1)S(1)} %copy-done.37, f32[2048,768]{1,0:T(8,128)S(1)} %get-tuple-element.220, f32[2048,768]{1,0:T(8,128)} %get-tuple-element.222, f32[768]{0:T(1024)S(1)} %copy-done.33), kind=kOutput, calls=%fused_computation.46 | convolution fusion | flops 2444229888 | bytes 23205888 | tf_op jit(solution)/shard_map/dot_general | solution.py:19
  241.5 4.0 convolution_convert_fusion
  245.6 8.6 %fusion.39 = f32[768,768]{1,0:T(8,128)} fusion(bf16[2048,768]{1,0:T(8,128)(2,1)} %copy-done.40, f32[768]{0:T(1024)} %convert_element_type.186, f32[768]{0:T(1024)S(1)} %convert_element_type.185, bf16[2048,768]{1,0:T(8,128)(2,1)} %all-reduce.8.cloned.1.call-done, bf16[2048,768]{1,0:T(8,128)(2,1)} %param.22, f32[2048]{0:T(1024)} %copy-done.24, ...), kind=kOutput, calls=%fused_computation.100 | convolution fusion | flops 2430074880 | bytes 11822080 | tf_op jit(solution)/shard_map/dot_general | solution.py:13
  254.2 60.1 %all-reduce.12.cloned.1.call-done = bf16[2048,768]{1,0:T(8,128)(2,1)} async-done(((bf16[2048,768]{1,0:T(8,128)(2,1)}), bf16[2048,768]{1,0:T(8,128)(2,1)}) %all-reduce.12.cloned.1.call-update) | async-done | bytes 3145744 | tf_op jit(solution)/shard_map/psum | solution.py:172
  314.2 9.8 %multiply_reduce_fusion.1 = (f32[768]{0:T(1024)S(1)}, f32[2048]{0:T(1024)S(1)}, f32[2048]{0:T(1024)S(1)}, f32[768]{0:T(1024)S(1)}, f32[768]{0:T(1024)S(1)}) fusion(f32[2048,768]{1,0:T(8,128)} %copy-done.6, bf16[2048,768]{1,0:T(8,128)(2,1)} %all-reduce.12.cloned.1.call-done, f32[2048]{0:T(1024)S(1)} %copy-done.25, f32[2048]{0:T(1024)S(1)} %broadcast_multiply_fusion.5, ...), kind=kLoop, calls=%fused_computation.47 | loop fusion | flops 25159424 | bytes 15776768 | tf_op jit(solution)/shard_map/reduce_sum | solution.py:38
  324.2 5.7 fusion.44
  337.5 33.8 %while.27 = (s32[]{:T(128)}, bf16[4,512,192]{1,2,0:T(8,128)(2,1)}, bf16[4,512,192]{1,2,0:T(8,128)(2,1)}, bf16[4,512,192]{1,2,0:T(8,128)(2,1)}, s32[4]{0:T(128)S(...) while((s32[]{:T(128)}, bf16[4,512,192]{1,2,0:T(8,128)(2,1)}, ...), condition=%wide.region_17.18_spmd, body=%wide.region_15.17_spmd.sunk | while | flops 510884864 | bytes 28344464 | solution.py:182
  381.2 8.0 %fusion.33 = f32[768,768]{1,0:T(8,128)} fusion(bf16[2048,768]{1,0:T(8,128)(2,1)} %copy-done.15, f32[2048,768]{1,0:T(8,128)} %copy-done.6), kind=kOutput, calls=%fused_computation.93 | convolution fusion | flops 2417491968 | bytes 11796480 | tf_op jit(solution)/shard_map/dot_general | solution.py:13
  397.4 37.7 %all-reduce = (f32[192]{0:T(256)}, f32[192]{0:T(256)}, f32[768]{0:T(1024)}, f32[768]{0:T(1024)}, f32[768]{0:T(1024)}, /*index=5*/f32[768]{0:T(1024)}, f32[768]{0:T(1024)}, f32[768]{0:T(1024)}, f32[768]{0:T(1024)}) all-reduce(f32[192]{0:T(256)S(1)} %convert_reduce_fusion.3, ...), channel_id=1, replica_groups=mesh['dp'=8,'mp'=4] {'dp'}, use_global_device_ids=true, to_apply=%region_21.22 | all-reduce | flops 5760 | bytes 46080 | tf_op jit(solution)/shard_map/psum | solution.py:209
  435.1 14.5 %all-reduce.14.cloned.1.call-done = bf16[2048,768]{1,0:T(8,128)(2,1)} async-done(((bf16[2048,768]{1,0:T(8,128)(2,1)}), bf16[2048,768]{1,0:T(8,128)(2,1)}) %all-reduce.14.cloned.1.call-update) | async-done | bytes 3145744 | tf_op jit(solution)/shard_map/psum | solution.py:207
  449.6 6.1 add_convert_fusion
  455.6 237.5 %all-reduce.16.cloned.1.call-done = (f32[768,192]{0,1:T(8,128)}, f32[768,192]{0,1:T(8,128)}, f32[768,192]{0,1:T(8,128)}, f32[192,768]{1,0:T(8,128)}, f32[768,768]{1,0:T(8,128)}, /*index=5*/f32[768,768]{1,0:T(8,128)}) async-done(((f32[768,192]{0,1:T(8,128)}, f32[768,192]{0,1:T(8,128)}, f32[768,192]{0,1:T(8,128)}, f32[192,768]{1,0:T(8,128)}, f32[768,768]{1,0:T(8,128)}, /*index=5*/f32[768,768]{1,0:T(8,128)}), ...) | async-done | bytes 7077904 | tf_op jit(solution)/shard_map/psum | solution.py:209
  (246 shorter events, 110.7 us)
Async XLA Ops:
  7.2 115.2 %copy-start = (bf16[768,768]{1,0:T(8,128)(2,1)S(1)}, bf16[768,768]{1,0:T(8,128)(2,1)}, u32[]{:S(2)}) copy-start(bf16[768,768]{1,0:T(8,128)(2,1)} %param.33) | copy-start | bytes 3538948
  7.2 108.7 %all-reduce.8.cloned.1.call-start = ((), (), s32[]{:S(2)}) async-start(), calls=%async_computation | async-start | bytes 6291456 | tf_op jit(solution)/shard_map/psum | solution.py:141
  38.8 5.9 copy-start.34
  38.8 6.0 copy-start.35
  44.7 170.7 %all-reduce.10.cloned.1.call-start = ((), (), s32[]{:S(2)}) async-start(), calls=%async_computation.1 | async-start | bytes 6291456 | tf_op jit(solution)/shard_map/psum | solution.py:153
  115.9 6.5 copy-start.29
  115.9 6.5 copy-start.32
  122.5 18.6 %copy-start.24 = (f32[2048]{0:T(1024)}, f32[2048]{0:T(1024)S(1)}, u32[]{:S(2)}) copy-start(f32[2048]{0:T(1024)S(1)} %add_rsqrt_fusion.1) | copy-start | bytes 24580
  122.5 20.3 %copy-start.36 = (bf16[768,768]{1,0:T(8,128)(2,1)S(1)}, bf16[768,768]{1,0:T(8,128)(2,1)}, u32[]{:S(2)}) copy-start(bf16[768,768]{1,0:T(8,128)(2,1)} %param.35) | copy-start | bytes 3538948
  146.7 167.5 %all-reduce.12.cloned.1.call-start = ((), (), s32[]{:S(2)}) async-start(), calls=%async_computation.2 | async-start | bytes 6291456 | tf_op jit(solution)/shard_map/psum | solution.py:172
  222.7 7.6 %slice-start.2 = ((s8[6291456]{0:T(1024)(128)(4,1)}), s8[4194304]{0:T(1024)(128)(4,1)S(1)}, s32[]{:S(2)}) async-start(s8[6291456]{0:T(1024)(128)(4,1)} %bitcast.200), calls=%async_computation.7 | async-start | bytes 8388608
  230.3 9.5 %copy-start.6 = (f32[2048,768]{1,0:T(8,128)}, f32[2048,768]{1,0:T(8,128)S(1)}, u32[]{:S(2)}) copy-start(f32[2048,768]{1,0:T(8,128)S(1)} %get-tuple-element.220) | copy-start | bytes 18874372
  245.5 68.7 %copy-start.25 = (f32[2048]{0:T(1024)S(1)}, f32[2048]{0:T(1024)}, u32[]{:S(2)}) copy-start(f32[2048]{0:T(1024)} %copy-done.24) | copy-start | bytes 24580
  245.6 204.0 %all-reduce.14.cloned.1.call-start = ((), (), s32[]{:S(2)}) async-start(), calls=%async_computation.3 | async-start | bytes 6291456 | tf_op jit(solution)/shard_map/psum | solution.py:207
  314.2 9.9 %copy-start.4 = (bf16[2048,768]{1,0:T(8,128)(2,1)S(1)}, bf16[2048,768]{1,0:T(8,128)(2,1)}, u32[]{:S(2)}) copy-start(bf16[2048,768]{1,0:T(8,128)(2,1)} %param.22) | copy-start | bytes 9437188
  314.2 9.9 %copy-start.9 = (bf16[2048,768]{1,0:T(8,128)(2,1)S(1)}, bf16[2048,768]{1,0:T(8,128)(2,1)}, u32[]{:S(2)}) copy-start(bf16[2048,768]{1,0:T(8,128)(2,1)} %all-reduce.8.cloned.1.call-done) | copy-start | bytes 9437188
  314.2 9.9 %copy-start.11 = (bf16[2048,768]{1,0:T(8,128)(2,1)S(1)}, bf16[2048,768]{1,0:T(8,128)(2,1)}, u32[]{:S(2)}) copy-start(bf16[2048,768]{1,0:T(8,128)(2,1)} %all-reduce.12.cloned.1.call-done) | copy-start | bytes 9437188
  324.1 8.3 %copy-start.18 = (bf16[192,768]{1,0:T(8,128)(2,1)S(1)}, bf16[192,768]{1,0:T(8,128)(2,1)}, u32[]{:S(2)}) copy-start(bf16[192,768]{1,0:T(8,128)(2,1)} %param.29) | copy-start | bytes 884740
  329.8 7.6 %copy-start.39 = (s32[4]{0:T(128)S(1)}, s32[4]{0:T(128)}, u32[]{:S(2)}) copy-start(s32[4]{0:T(128)} %param.23) | copy-start | bytes 52
  380.9 312.3 %all-reduce.16.cloned.1.call-start = ((), (), s32[]{:S(2)}) async-start(), calls=%async_computation.4 | async-start | bytes 14155776 | tf_op jit(solution)/shard_map/psum | solution.py:209
  381.2 8.0 %copy-start.5 = (bf16[2048,768]{1,0:T(8,128)(2,1)S(1)}, bf16[2048,768]{1,0:T(8,128)(2,1)}, u32[]{:S(2)}) copy-start(bf16[2048,768]{1,0:T(8,128)(2,1)} %param.22) | copy-start | bytes 9437188
  693.2 7.9 %copy-start.17 = (f32[768,768]{1,0:T(8,128)S(1)}, f32[768,768]{1,0:T(8,128)}, u32[]{:S(2)}) copy-start(f32[768,768]{1,0:T(8,128)} %get-tuple-element.415) | copy-start | bytes 7077892
  693.2 9.3 %copy-start.16 = (f32[768,768]{1,0:T(8,128)S(1)}, f32[768,768]{1,0:T(8,128)}, u32[]{:S(2)}) copy-start(f32[768,768]{1,0:T(8,128)} %get-tuple-element.417) | copy-start | bytes 7077892
  693.2 10.7 %copy-start.1 = (bf16[768,768]{1,0:T(8,128)(2,1)S(1)}, bf16[768,768]{1,0:T(8,128)(2,1)}, u32[]{:S(2)}) copy-start(bf16[768,768]{1,0:T(8,128)(2,1)} %param.33) | copy-start | bytes 3538948
  (26 other events, 89.5 us)
Sparse Core Ops, SparseCore 0:
  44.8 71.1 all-reduce.7
  146.8 68.5 all-reduce.9
  245.7 68.5 all-reduce.11
  381.0 68.5 all-reduce.13
  455.7 237.4 all-reduce.15
where the time goes:
time: 720 us; the launch traced here: 711 us
  waiting for transfers between devices  445 us (62%)
  matrix products  97.6 us (14%)
  other arithmetic  64.7 us (9%)
  local copies, waits for them, and re-layouts  49.6 us (7%)
  blocking collectives  37.7 us (5%)
  between operations  14.8 us (2%)
    psum x1, waiting for transfers between devices, shards(): lax.psum((query_weight_grad, query_bias_grad, key_weight_grad, value_weig...  238 us
    psum x1, waiting for transfers between devices, shards(): lax.psum(jnp.dot(attended, out_weight, preferred_element_type=jnp.float32...  68.6 us
    psum x1, waiting for transfers between devices, shards(): lax.psum(jnp.dot(activated, down_weight, preferred_element_type=jnp.float...  64.6 us
    psum x1, waiting for transfers between devices, shards(): lax.psum(inner_cols(grad_hidden, up_weight).astype(jnp.bfloat16), 'mp')  60.1 us
    psum x1, blocking collectives, shards(): lax.psum((query_weight_grad, query_bias_grad, key_weight_grad, value_weig...  37.7 us
    dot_general x6, matrix products, outer_rows(): lax.dot_general(left, right, (((0,), (0,)), ((), ())), preferred_element_...  23.1 us
    dot_general x6, matrix products, inner_cols(): lax.dot_general(left, right, (((1,), (1,)), ((), ())), preferred_element_...  20.5 us
    unnamed x96, local copies, waits for them, and re-layouts  19.3 us
  transfers between devices with their start and end apart: 5, of which 5 were waited for; matrix products, arithmetic and copies ran while one was open for 5% of the time, Pallas kernels for 0%

commit v1 on v0

v1 whole, which is shorter than its diff:
```python
import jax
import jax.numpy as jnp
from jax import lax
from jax.sharding import PartitionSpec as P

HD = 64
EPS = 1e-06
BF = jnp.bfloat16
F32 = jnp.float32


def mm(a, b, ca, cb):
    return lax.dot_general(a, b, (((ca,), (cb,)), ((), ())), preferred_element_type=F32)


def split_heads(row_block):
    return row_block.reshape(row_block.shape[0], -1, HD).transpose(1, 0, 2)


def join_heads(head_block):
    return head_block.transpose(1, 0, 2).reshape(head_block.shape[1], -1)


def norm_parts(rows):
    center = rows - jnp.mean(rows, axis=-1, keepdims=True)
    inv = lax.rsqrt(jnp.mean(center * center, axis=-1, keepdims=True) + EPS)
    return center * inv, inv


def norm_back(up, normed, inv, gain):
    c = up * gain
    return inv * (
        c
        - jnp.mean(c, axis=-1, keepdims=True)
        - normed * jnp.mean(c * normed, axis=-1, keepdims=True)
    )


def attend_forward(pieces):
    q, k, v, length = pieces
    s = jnp.einsum("hqd,hkd->hqk", split_heads(q), split_heads(k), preferred_element_type=F32)
    live = lax.iota(jnp.int32, k.shape[0]) < length
    s = jnp.where(live[None, None, :], s, -1e30)
    e = jnp.exp(s - jnp.max(s, axis=-1, keepdims=True)).astype(BF)
    rinv = 1.0 / jnp.sum(e.astype(F32), axis=-1, keepdims=True)
    o = jnp.einsum("hqk,hkd->hqd", e, split_heads(v), preferred_element_type=F32) * rinv
    return join_heads(o).astype(BF), e, rinv


def attend_back(pieces):
    q, k, v, e, rinv, o, do = pieces
    qh, kh, vh = split_heads(q), split_heads(k), split_heads(v)
    doh = split_heads(do).astype(F32) * rinv
    d = jnp.sum(doh * split_heads(o).astype(F32), axis=-1, keepdims=True)
    dol = doh.astype(BF)
    dv = jnp.einsum("hqk,hqd->hkd", e, dol, preferred_element_type=F32)
    dp = jnp.einsum("hqd,hkd->hqk", dol, vh, preferred_element_type=F32)
    ds = (e.astype(F32) * (dp - d)).astype(BF)
    dq = jnp.einsum("hqk,hkd->hqd", ds, kh, preferred_element_type=F32) * HD ** (-0.5)
    dk = jnp.einsum("hqk,hqd->hkd", ds, qh, preferred_element_type=F32)
    return join_heads(dq).astype(BF), join_heads(dk).astype(BF), join_heads(dv).astype(BF)


def shards(
    tokens, lengths, wq, bq, wk, wv, bv, wo, bo, g1, s1, wu, bu, wd, bd, g2, s2, cot
):
    n = lengths.shape[0]
    rows = tokens.shape[0]
    seq = rows // n
    m = lax.axis_index("mp")
    own = lambda a: lax.dynamic_slice_in_dim(a, m * seq, seq, 0)
    f = lambda a: a.astype(F32)

    def by_table(a):
        return a.reshape(n, seq, a.shape[1])

    q = ((mm(tokens, wq, 1, 0) + f(bq)).astype(BF) * HD ** (-0.5)).astype(BF)
    k = mm(tokens, wk, 1, 0).astype(BF)
    v = (mm(tokens, wv, 1, 0) + f(bv)).astype(BF)
    att, e, rinv = lax.map(attend_forward, (by_table(q), by_table(k), by_table(v), lengths))
    att_own = lax.all_to_all(att, "mp", 0, 0)
    wo_all = lax.all_gather(wo, "mp")
    wu_all = lax.all_gather(wu, "mp")
    wd_all = lax.all_gather(wd, "mp")
    bu_all = lax.all_gather(f(bu), "mp")
    mixed = (
        f(own(tokens))
        + jnp.einsum("qtk,qkd->td", att_own, wo_all, preferred_element_type=F32)
        + f(bo)
    )
    n1, i1 = norm_parts(mixed)
    first = n1 * f(g1) + f(s1)
    first_low = first.astype(BF)
    hidden = (
        jnp.einsum("td,qdf->qtf", first_low, wu_all, preferred_element_type=F32)
        + bu_all[:, None, :]
    )
    act, gelu_pull = jax.vjp(lambda h: jax.nn.gelu(h, approximate=False), hidden)
    act = act.astype(BF)
    second = first + jnp.einsum("qtf,qfd->td", act, wd_all, preferred_element_type=F32) + f(bd)
    n2, i2 = norm_parts(second)
    out_own = (n2 * f(g2) + f(s2)).astype(BF)
    c_own = f(own(cot))
    d2 = norm_back(c_own, n2, i2, f(g2))
    d2l = d2.astype(BF)
    dg2, ds2, dbd = jnp.sum(c_own * n2, 0), jnp.sum(c_own, 0), jnp.sum(d2, 0)
    dwd = jnp.einsum("qtf,td->qfd", act, d2l, preferred_element_type=F32)
    dact = jnp.einsum("td,qfd->qtf", d2l, wd_all, preferred_element_type=F32)
    dh = gelu_pull(dact)[0].astype(BF)
    dbu = jnp.sum(f(dh), axis=1)
    dwu = jnp.einsum("td,qtf->qdf", first_low, dh, preferred_element_type=F32)
    d1 = d2 + jnp.einsum("qtf,qdf->td", dh, wu_all, preferred_element_type=F32)
    dg1, ds1 = jnp.sum(d1 * n1, 0), jnp.sum(d1, 0)
    dm = norm_back(d1, n1, i1, f(g1))
    dbo = jnp.sum(dm, 0)
    dml = dm.astype(BF)
    dwo = jnp.einsum("qtk,td->qkd", att_own, dml, preferred_element_type=F32)
    datt = jnp.einsum("td,qkd->qtk", dml, wo_all, preferred_element_type=F32).astype(BF)
    datt = lax.all_to_all(datt, "mp", 0, 0)
    dq, dk, dv = lax.map(
        attend_back, (by_table(q), by_table(k), by_table(v), e, rinv, att, datt)
    )
    dq, dk, dv = (a.reshape(rows, -1) for a in (dq, dk, dv))
    dbq, dbv = jnp.sum(f(dq), 0), jnp.sum(f(dv), 0)
    dwq, dwk, dwv = (mm(tokens, a, 0, 0) for a in (dq, dk, dv))
    back = (mm(dq, wq, 1, 1) + mm(dk, wk, 1, 1) + mm(dv, wv, 1, 1)).astype(BF)
    back = jnp.sum(f(lax.all_to_all(back.reshape(n, seq, -1), "mp", 0, 0)), 0)
    tg_own = (dm + back).astype(BF)
    layer_out = lax.all_gather(out_own, "mp", tiled=True)
    tokens_grad = lax.all_gather(tg_own, "mp", tiled=True)
    low = lambda a: a.astype(BF)
    ffn = lax.psum_scatter(jnp.stack([low(dwu), low(dwd)], 1), "mp", scatter_dimension=0)
    dwo = lax.psum_scatter(low(dwo), "mp", scatter_dimension=0)
    dbu = lax.psum_scatter(dbu, "mp", scatter_dimension=0)
    dwq, dwk, dwv, dwo, ffn = lax.psum((low(dwq), low(dwk), low(dwv), dwo, ffn), "dp")
    dbq, dbv, dbu = lax.psum((dbq, dbv, dbu), "dp")
    dbo, dg1, ds1, dbd, dg2, ds2 = lax.psum((dbo, dg1, ds1, dbd, dg2, ds2), ("dp", "mp"))
    return (
        layer_out, tokens_grad, f(dwq), dbq, f(dwk), f(dwv), dbv, f(dwo), dbo, dg1, ds1,
        f(ffn[0]), dbu, f(ffn[1]), dbd, dg2, ds2,
    )


def solution(mesh):
    row, col, one, rep = P("dp", None), P(None, "mp"), P("mp"), P()
    low = P("mp", None)
    in_specs = (
        row, P("dp"), col, one, col, col, one, low, rep, rep, rep, col, one, low, rep, rep, rep, row,
    )
    out_specs = (
        row, row, col, one, col, col, one, low, rep, rep, rep, col, one, low, rep, rep, rep,
    )
    return jax.shard_map(shards, mesh=mesh, in_specs=in_specs, out_specs=out_specs, check_vma=False)
```

time: 720 us -> 625 us (0.87); the launches traced: 711 us -> 623 us
  waiting for transfers between devices: 445 us -> 235 us
  blocking collectives: 37.7 us -> 166 us
  other arithmetic: 64.7 us -> 33.8 us
  local copies, waits for them, and re-layouts: 49.6 us -> 76 us
  matrix products: 97.6 us -> 88.1 us
  starting transfers between devices: 0.63 us -> 8.72 us
    psum x5 -> x1, waiting for transfers between devices: 445 us -> 134 us  [shards(): lax.psum((low(dwq), low(dwk), low(dwv), dwo, ffn), 'dp')]
    all_to_all x0 -> x1, blocking collectives: none -> 70.7 us  [shards(): back = jnp.sum(f(lax.all_to_all(back.reshape(n, seq, -1), 'mp', 0, 0)), 0)]
    unnamed x5 -> x9, waiting for transfers between devices: 0.08 us -> 38.3 us
    reduce_sum x13 -> x16, other arithmetic: 35.6 us -> 5.6 us  [the longest x2 2.37 us: shards(): dg2, ds2, dbd = (jnp.sum(c_own * n2, 0), jnp.sum(c_own, 0), jnp.sum(d2, 0))]
    dynamic_slice x32 -> x40, local copies, waits for them, and re-layouts: 8.9 us -> 38.8 us  [the longest x32 29.8 us: shards(): lax.map(attend_forward, (by_table(q), by_table(k), by_table(v), lengths))]
    psum x1 -> x2, blocking collectives: 37.7 us -> 63.5 us  [the longest x1 41.6 us: shards(): lax.psum((dbo, dg1, ds1, dbd, dg2, ds2), ('dp', 'mp'))]
    reduce_scatter x0 -> x1, waiting for transfers between devices: none -> 24.8 us  [shards(): dwo = lax.psum_scatter(low(dwo), 'mp', scatter_dimension=0)]
    all_gather x0 -> x1, blocking collectives: none -> 22.1 us  [shards(): bu_all = lax.all_gather(f(bu), 'mp')]
  transfers between devices with their start and end apart: 5 -> 10, of which waited for: 5 -> 5; matrix products, arithmetic and copies ran while one was open for 5% -> 23% of each run, Pallas kernels for 0% -> 0%
where the time goes in v1:
time: 625 us; the launch traced here: 623 us
  waiting for transfers between devices  235 us (38%)
  blocking collectives  166 us (27%)
  matrix products  88.1 us (14%)
  local copies, waits for them, and re-layouts  76 us (12%)
  other arithmetic  33.8 us (5%)
  between operations  14.8 us (2%)
  starting transfers between devices  8.72 us (1%)
    psum x1, waiting for transfers between devices, shards(): lax.psum((low(dwq), low(dwk), low(dwv), dwo, ffn), 'dp')  134 us
    all_to_all x1, blocking collectives, shards(): back = jnp.sum(f(lax.all_to_all(back.reshape(n, seq, -1), 'mp', 0, 0)), 0)  70.7 us
    psum x1, blocking collectives, shards(): lax.psum((dbo, dg1, ds1, dbd, dg2, ds2), ('dp', 'mp'))  41.6 us
    unnamed x9, waiting for transfers between devices  38.3 us
    dynamic_slice x32, local copies, waits for them, and re-layouts, shards(): lax.map(attend_forward, (by_table(q), by_table(k), by_table(v), lengths))  29.8 us
    reduce_scatter x1, waiting for transfers between devices, shards(): dwo = lax.psum_scatter(low(dwo), 'mp', scatter_dimension=0)  24.8 us
    all_gather x1, blocking collectives, shards(): bu_all = lax.all_gather(f(bu), 'mp')  22.1 us
    psum x1, blocking collectives, shards(): dbq, dbv, dbu = lax.psum((dbq, dbv, dbu), 'dp')  21.9 us
  transfers between devices with their start and end apart: 10, of which 5 were waited for; matrix products, arithmetic and copies ran while one was open for 23% of the time, Pallas kernels for 0%

profile of v1, /device:TPU:0, one launch (start us, length us, event | category | flops | bytes accessed | tf_op | source)
XLA Modules:
  0.0 623.3 jit_solution(16745428390254472767)
XLA Ops:
  19.7 28.2 %while.28 = (s32[]{:T(128)}, bf16[4,512,192]{1,2,0:T(8,128)(2,1)}, bf16[4,3,512,512]{2,3,1,0:T(8,128)(2,1)}, f32[4,3,512,1]{2,1,3,0:T(4,128)S(1)}, s32[4]{0:T(12...) while((s32[]{:T(128)}, bf16[4,512,192]{1,2,0:T(8,128)(2,1)}, ...), condition=%wide.region_3.4_spmd, body=%wide.region_0.3_spmd.sunk | while | flops 207028736 | bytes 14998137 | solution.py:80
  47.8 4.2 all-to-all-start
  52.2 22.1 %all-gather.4 = f32[4,1,768]{2,1,0:T(1,128)S(1)} all-gather(f32[1,1,768]{2,1,0:T(1,128)S(1)} %reshape.227), channel_id=4, replica_groups=mesh['dp'=8,'mp'=4] {'mp'}, dimensions={0}, use_global_device_ids=true | all-gather | bytes 15360 | tf_op jit(solution)/shard_map/all_gather | solution.py:85
  78.3 20.4 %fusion.24 = (bf16[4,512,768]{2,1,0:T(8,128)(2,1)}, f32[4,512,768]{2,1,0:T(8,128)}, f32[512,4,768]{2,0,1:T(8,128)}) fusion(f32[4,768]{1,0:T(4,128)S(1)} %bitcast.374, bf16[4,768,768]{2,1,0:T(8,128)(2,1)} %bitcast.376, f32[512,768]{1,0:T(8,128)} %copy-done.15, f32[768]{0:T(1024)S(1)} %convert_element_type.242, f32[768]{0:T(1024)S(1)} %convert_element_type.241, ...), kind=kOutput, calls=%fused_computation.56 | convolution fusion | flops 2521694208 | bytes 22042624 | tf_op jit(solution)/shard_map/td,qdf->qtf/dot_general | solution.py:95
  98.7 17.8 %all-gather.19.cloned.1.call-done = bf16[3072,768]{1,0:T(8,128)(2,1)} async-done(((bf16[768,768]{1,0:T(8,128)(2,1)}), bf16[3072,768]{1,0:T(8,128)(2,1)}) %all-gather.19.cloned.1.call-update) | async-done | bytes 4718608 | tf_op jit(solution)/shard_map/all_gather | solution.py:84
  116.4 6.8 %fusion.73 = (f32[512]{0:T(512)S(1)}, f32[512,768]{1,0:T(8,128)S(1)}) fusion(f32[768]{0:T(1024)S(1)} %convert_element_type.245, bf16[4,512,768]{2,1,0:T(8,128)(2,1)} %get-tuple-element.300, bf16[4,768,768]{2,1,0:T(8,128)(2,1)} %bitcast.378, f32[768]{0:T(1024)S(1)} %convert_element_type.242, f32[768]{0:T(1024)S(1)} %convert_element_type.241, ...), kind=kOutput, calls=%fused_computation.150 | convolution fusion | flops 2418671104 | bytes 11025408 | tf_op jit(solution)/shard_map/qtf,qfd->td/dot_general | solution.py:100
  126.0 4.4 convert_bitcast_fusion.2
  130.4 6.8 %convert_reduce_fusion.1 = (f32[4,768]{1,0:T(4,128)S(1)}, bf16[4,512,768]{2,1,0:T(8,128)(2,1)S(1)}) fusion(f32[4,512,768]{2,1,0:T(8,128)S(1)} %bitcast.385, bf16[4,768,768]{2,1,0:T(8,128)(2,1)S(1)} %bitcast.381, f32[512,768]{1,0:T(8,128)S(1)} %get-tuple-element.297, f32[512,4,768]{2,0,1:T(8,128)} %get-tuple-element.313, f32[4,768]{1,0:T(4,128)S(1)} %bitcast.375), kind=kOutput, calls=%fused_computation.57 | convolution fusion | flops 2443047936 | bytes 22044672 | tf_op jit(solution)/shard_map/td,qfd->qtf/dot_general | solution.py:108
  138.9 4.6 convert_bitcast_fusion.3
  143.4 8.3 %pad_maximum_fusion = bf16[4,2,768,768]{2,3,0,1:T(8,128)(2,1)} fusion(bf16[4,1,768,768]{2,3,0,1:T(8,128)(2,1)} %convert_bitcast_fusion.2, bf16[4,1,768,768]{2,3,0,1:T(8,128)(2,1)} %convert_bitcast_fusion.3), kind=kLoop, calls=%fused_computation.39 | loop fusion | flops 4718592 | bytes 18874368 | tf_op jit(solution)/shard_map/stack | solution.py:132
  151.8 6.3 %multiply_reduce_fusion = (f32[768]{0:T(1024)S(1)}, f32[512]{0:T(512)S(1)}, f32[512]{0:T(512)S(1)}, f32[768]{0:T(1024)S(1)}, f32[512,768]{1,0:T(8,128)S(1)}) fusion(f32[512,768]{1,0:T(8,128)S(1)} %copy-done.16, f32[512]{0:T(512)S(1)} %add_rsqrt_fusion.1, f32[512]{0:T(512)S(1)} %broadcast_multiply_fusion.5, f32[768]{0:T(1024)S(1)} %convert_element_type.241, ...), kind=kOutput, calls=%fused_computation.97 | convolution fusion | flops 2419848704 | bytes 12600320 | tf_op jit(solution)/shard_map/qtf,qdf->td/dot_general | solution.py:112
  158.7 3.5 convolution_convert_fusion.2
  163.9 4.2 all-to-all-start.1
  168.7 19.8 %all-to-all-done.1 = bf16[4,512,192]{1,2,0:T(8,128)(2,1)} async-done(((bf16[4,512,192]{1,2,0:T(8,128)(2,1)}), bf16[4,512,192]{1,2,0:T(8,128)(2,1)}, u32[]{:S(2)}, u32[]{:S(2)}) %all-to-all-start.1) | async-done | bytes 786464 | tf_op jit(solution)/shard_map/all_to_all | solution.py:119
  191.5 47.6 %while.29 = (s32[]{:T(128)}, bf16[4,512,192]{1,2,0:T(8,128)(2,1)}, bf16[4,512,192]{1,2,0:T(8,128)(2,1)}, bf16[4,512,192]{1,2,0:T(8,128)(2,1)}, bf16[4,3,512,512]...) while((s32[]{:T(128)}, bf16[4,512,192]{1,2,0:T(8,128)(2,1)}, ...), condition=%wide.region_14.15_spmd, body=%wide.region_12.14_spmd.sunk | while | flops 407271936 | bytes 20884680 | solution.py:120
  245.4 70.7 %all_to_all.15 = bf16[4,512,768]{2,1,0:T(8,128)(2,1)S(1)} all-to-all(bf16[4,512,768]{2,1,0:T(8,128)(2,1)S(1)} %bitcast.359), channel_id=1, replica_groups=mesh['dp'=8,'mp'=4] {'mp'}, dimensions={0} | all-to-all | bytes 6291456 | tf_op jit(solution)/shard_map/all_to_all | solution.py:127
  325.4 35.6 %all-reduce.8.cloned.1.call-done = bf16[4,2,768,768]{2,3,0,1:T(8,128)(2,1)} async-done(((bf16[4,2,768,768]{2,3,0,1:T(8,128)(2,1)}), bf16[4,2,768,768]{2,3,0,1:T(8,128)(2,1)}) %all-reduce.8.cloned.1.call-update) | async-done | bytes 9437200
  361.0 3.9 dynamic-slice_bitcast_fusion.1
  365.0 24.8 %reduce-scatter.5.cloned.1.call-done = bf16[1,192,768]{2,1,0:T(8,128)(2,1)} async-done(((bf16[4,192,768]{2,1,0:T(8,128)(2,1)}), bf16[1,192,768]{2,1,0:T(8,128)(2,1)}) %reduce-scatter.5.cloned.1.call-update) | async-done | bytes 294928 | tf_op jit(solution)/shard_map/reduce_scatter | solution.py:133
  389.8 10.1 %all-reduce.1 = f32[4,768]{1,0:T(4,128)S(1)} all-reduce(f32[4,768]{1,0:T(4,128)S(1)} %get-tuple-element.317), channel_id=8, replica_groups=mesh['dp'=8,'mp'=4] {'mp'}, use_global_device_ids=true, to_apply=%region_34.35.clone | all-reduce | flops 3072 | bytes 24576
  400.6 41.6 %all-reduce.2 = (f32[768]{0:T(1024)}, f32[768]{0:T(1024)}, f32[768]{0:T(1024)}, f32[768]{0:T(1024)}, f32[768]{0:T(1024)}, /*index=5*/f32[768]{0:T(1024)}) all-reduce(f32[768]{0:T(1024)S(1)} %get-tuple-element.298, f32[768]{0:T(1024)S(1)} %get-tuple-element.237, ...), channel_id=1, replica_groups=mesh['dp'=8,'mp'=4] {'dp','mp'}, use_global_device_ids=true, to_apply=%region_26.27 | all-reduce | flops 4608 | bytes 36864 | tf_op jit(solution)/shard_map/psum | solution.py:137
  442.5 21.9 %all-reduce.3 = (f32[192]{0:T(256)}, f32[192]{0:T(256)}, f32[768]{0:T(1024)}) all-reduce(f32[192]{0:T(256)S(1)} %convert_reduce_fusion.5, f32[192]{0:T(256)S(1)} %convert_reduce_fusion.4, f32[768]{0:T(1024)S(1)} %dynamic-slice_reduce_fusion), channel_id=1, replica_groups=mesh['dp'=8,'mp'=4] {'dp'}, use_global_device_ids=true, to_apply=%region_18.19 | all-reduce | flops 1152 | bytes 9216 | tf_op jit(solution)/shard_map/psum | solution.py:136
  464.4 134.4 %all-reduce.10.cloned.1.call-done = (bf16[768,192]{0,1:T(8,128)(2,1)}, bf16[768,192]{0,1:T(8,128)(2,1)}, bf16[768,192]{0,1:T(8,128)(2,1)}, bf16[192,768]{1,0:T(8,128)(2,1)}, bf16[2,768,768]{1,2,0:T(8,128)(2,1)}) async-done(((bf16[768,192]{0,1:T(8,128)(2,1)}, bf16[768,192]{0,1:T(8,128)(2,1)}, bf16[768,192]{0,1:T(8,128)(2,1)}, bf16[192,768]{1,0:T(8,128)(2,1)}, bf16[2,768,768]{1,2,0:T(8,128)(2,1)}), ...) | async-done | bytes 3538960 | tf_op jit(solution)/shard_map/psum | solution.py:135
  598.9 3.4 fusion.51
  (282 shorter events, 132.5 us)
Async XLA Ops:
  7.2 6.8 %copy-start = (bf16[768,192]{0,1:T(8,128)(2,1)S(1)}, bf16[768,192]{0,1:T(8,128)(2,1)}, u32[]{:S(2)}) copy-start(bf16[768,192]{0,1:T(8,128)(2,1)} %param.24) | copy-start | bytes 884740
  7.2 67.1 %all-gather.15.cloned.1.call-start = ((), (), s32[]{:S(2)}) async-start(), calls=%async_computation.7 | async-start | bytes 1474560 | tf_op jit(solution)/shard_map/all_gather | solution.py:82
  7.9 70.3 %all-gather.17.cloned.1.call-start = ((), (), s32[]{:S(2)}) async-start(), calls=%async_computation.8 | async-start | bytes 5898240 | tf_op jit(solution)/shard_map/all_gather | solution.py:83
  8.7 107.7 %all-gather.19.cloned.1.call-start = ((), (), s32[]{:S(2)}) async-start(), calls=%async_computation.9 | async-start | bytes 5898240 | tf_op jit(solution)/shard_map/all_gather | solution.py:84
  19.6 32.5 %copy-start.26 = (bf16[768]{0:T(1024)(128)(2,1)S(1)}, bf16[768]{0:T(1024)(128)(2,1)}, u32[]{:S(2)}) copy-start(bf16[768]{0:T(1024)(128)(2,1)} %param.30) | copy-start | bytes 4612
  19.6 32.5 %copy-start.27 = (bf16[768]{0:T(1024)(128)(2,1)S(1)}, bf16[768]{0:T(1024)(128)(2,1)}, u32[]{:S(2)}) copy-start(bf16[768]{0:T(1024)(128)(2,1)} %param.31) | copy-start | bytes 4612
  19.6 32.5 %copy-start.28 = (bf16[768]{0:T(1024)(128)(2,1)S(1)}, bf16[768]{0:T(1024)(128)(2,1)}, u32[]{:S(2)}) copy-start(bf16[768]{0:T(1024)(128)(2,1)} %param.32) | copy-start | bytes 4612
  19.6 32.6 %copy-start.32 = (bf16[768]{0:T(1024)(128)(2,1)S(1)}, bf16[768]{0:T(1024)(128)(2,1)}, u32[]{:S(2)}) copy-start(bf16[768]{0:T(1024)(128)(2,1)} %param.34) | copy-start | bytes 4612
  19.6 54.6 %copy-start.29 = (bf16[768]{0:T(1024)(128)(2,1)S(1)}, bf16[768]{0:T(1024)(128)(2,1)}, u32[]{:S(2)}) copy-start(bf16[768]{0:T(1024)(128)(2,1)} %param.36) | copy-start | bytes 4612
  19.6 54.6 %copy-start.30 = (bf16[768]{0:T(1024)(128)(2,1)S(1)}, bf16[768]{0:T(1024)(128)(2,1)}, u32[]{:S(2)}) copy-start(bf16[768]{0:T(1024)(128)(2,1)} %param.37) | copy-start | bytes 4612
  19.7 54.6 %copy-start.31 = (bf16[768]{0:T(1024)(128)(2,1)S(1)}, bf16[768]{0:T(1024)(128)(2,1)}, u32[]{:S(2)}) copy-start(bf16[768]{0:T(1024)(128)(2,1)} %param.38) | copy-start | bytes 4612
  47.8 26.5 %all-to-all-start = ((bf16[4,512,192]{1,2,0:T(8,128)(2,1)}), bf16[4,512,192]{1,2,0:T(8,128)(2,1)}, u32[]{:S(2)}, u32[]{:S(2)}) async-start(bf16[4,512,192]{1,2,0:T(8,128)(2,1)} %get-tuple-element.488), calls=%async_computation | async-start | bytes 1572864 | tf_op jit(solution)/shard_map/all_to_all | solution.py:81
  52.1 308.9 %all-reduce.8.cloned.1.call-start = ((), (), s32[]{:S(2)}) async-start(), calls=%async_computation.10 | async-start | bytes 18874368
  78.3 38.2 %copy-start.16 = (f32[512,768]{1,0:T(8,128)S(1)}, f32[512,768]{1,0:T(8,128)}, u32[]{:S(2)}) copy-start(f32[512,768]{1,0:T(8,128)} %copy-done.15) | copy-start | bytes 4718596
  116.4 7.1 %copy-start.19 = (bf16[2048,768]{1,0:T(8,128)(2,1)S(1)}, bf16[2048,768]{1,0:T(8,128)(2,1)}, u32[]{:S(2)}) copy-start(bf16[2048,768]{1,0:T(8,128)(2,1)} %param.39) | copy-start | bytes 9437188
  124.4 6.0 slice-start
  124.4 6.0 slice-start.2
  151.7 238.0 %reduce-scatter.5.cloned.1.call-start = ((), (), s32[]{:S(2)}) async-start(), calls=%async_computation.6 | async-start | bytes 1474560 | tf_op jit(solution)/shard_map/reduce_scatter | solution.py:133
  163.9 24.7 %all-to-all-start.1 = ((bf16[4,512,192]{1,2,0:T(8,128)(2,1)}), bf16[4,512,192]{1,2,0:T(8,128)(2,1)}, u32[]{:S(2)}, u32[]{:S(2)}) async-start(bf16[4,512,192]{1,2,0:T(8,128)(2,1)} %fusion.50), calls=%async_computation.1 | async-start | bytes 1572864 | tf_op jit(solution)/shard_map/all_to_all | solution.py:119
  168.1 296.3 %all-gather.11.cloned.1.call-start = ((), (), s32[]{:S(2)}) async-start(), calls=%async_computation.4 | async-start | bytes 3932160 | tf_op jit(solution)/shard_map/all_gather | solution.py:129
  168.7 295.7 %all-gather.13.cloned.1.call-start = ((), (), s32[]{:S(2)}) async-start(), calls=%async_computation.5 | async-start | bytes 3932160 | tf_op jit(solution)/shard_map/all_gather | solution.py:130
  318.5 280.4 %all-reduce.10.cloned.1.call-start = ((), (), s32[]{:S(2)}) async-start(), calls=%async_computation.11 | async-start | bytes 7077888 | tf_op jit(solution)/shard_map/psum | solution.py:135
  361.0 81.1 %copy-start.14 = (bf16[4,512,192]{1,2,0:T(8,128)(2,1)S(1)}, bf16[4,512,192]{1,2,0:T(8,128)(2,1)}, u32[]{:S(2)}) copy-start(bf16[4,512,192]{1,2,0:T(8,128)(2,1)} %get-tuple-element.125) | copy-start | bytes 2359300
  365.0 77.4 %copy-start.12 = (bf16[4,512,192]{1,2,0:T(8,128)(2,1)S(1)}, bf16[4,512,192]{1,2,0:T(8,128)(2,1)}, u32[]{:S(2)}) copy-start(bf16[4,512,192]{1,2,0:T(8,128)(2,1)} %get-tuple-element.123) | copy-start | bytes 2359300
  (34 other events, 93.9 us)
Sparse Core Ops, SparseCore 0:
  9.6 20.1 all-gather.14
  31.3 45.9 all-gather.16
  78.9 37.4 all-gather.18
  151.9 209.1 all-reduce.7
  364.0 25.7 reduce-scatter.4
  391.2 29.2 all-gather.10
  422.7 29.1 all-gather.12
  457.8 141.0 all-reduce.9

commit v2 on v1

v2 whole, which is shorter than its diff:
```python
import functools

import jax
import jax.numpy as jnp
from jax import lax
from jax.experimental import pallas as pl
from jax.experimental.pallas import tpu as pltpu
from jax.sharding import PartitionSpec as P

HD = 64
EPS = 1e-06
BF = jnp.bfloat16
F32 = jnp.float32
MESH = pl.DeviceIdType.MESH


def mm(a, b, ca, cb):
    return lax.dot_general(a, b, (((ca,), (cb,)), ((), ())), preferred_element_type=F32)


def flip(v, b):
    return v + b - 2 * b * lax.rem(v // b, 2)


def gelu_pair(h):
    x = h * 0.7071067811865476
    e = jnp.exp(-(x * x))
    t = 1.0 / (1.0 + 0.3275911 * jnp.abs(x))
    poly = t * (
        0.254829592
        + t * (-0.284496736 + t * (1.421413741 + t * (-1.453152027 + t * 1.061405429)))
    )
    tail = 0.5 * poly * e
    phi = jnp.where(h > 0, 1.0 - tail, tail)
    return h * phi, phi + h * e * 0.3989422804014327


def norm_rows(x):
    center = x - jnp.mean(x, axis=-1, keepdims=True)
    inv = lax.rsqrt(jnp.mean(center * center, axis=-1, keepdims=True) + EPS)
    return center * inv, inv


class Comm:
    def __init__(self, nbits):
        self.dp, self.mp = lax.axis_index("dp"), lax.axis_index("mp")
        self.nbits = nbits

    def mpeer(self, k):
        v = self.mp
        for b in (1, 2):
            if k & b:
                v = flip(v, b)
        return (self.dp, v)

    def dpeer(self, bit):
        return (flip(self.dp, 1 << bit), self.mp)

    def barrier(self):
        bar = pltpu.get_barrier_semaphore()
        peers = [self.mpeer(k) for k in (1, 2, 3)] + [self.dpeer(b) for b in range(self.nbits)]
        for p in peers:
            pl.semaphore_signal(bar, inc=1, device_id=p, device_id_type=MESH)
        pl.semaphore_wait(bar, len(peers))


def rcopy(src, dst, ss, rs, dev):
    return pltpu.make_async_remote_copy(
        src_ref=src, dst_ref=dst, send_sem=ss, recv_sem=rs, device_id=dev, device_id_type=MESH
    )


def fwd_kernel(nbits, names, *refs):
    r = dict(zip(names, refs))
    ln, vec, tok = r["len"], r["vec"], r["tok"]
    TOK, WT, QT, KT, VT, ET, RI = (r[k] for k in ("TOK", "WT", "QT", "KT", "VT", "ET", "RI"))
    ATQ, ATO, N1, I1, FL, ACT, GP = (r[k] for k in ("ATQ", "ATO", "N1", "I1", "FL", "ACT", "GP"))
    WA = (r["WOA"], r["UA"], r["DA"])
    VA, FIRST, ACC, N2, I2 = (r[k] for k in ("VA", "FIRST", "ACC", "N2", "I2"))
    wsrc = (r["wo"], r["wu"], r["wd"])
    c = Comm(nbits)
    m = c.mp
    seq, d = TOK.shape[1], TOK.shape[2]
    hw = VT.shape[1]
    nh = hw // HD
    aug = QT.shape[2]

    lc = []
    for i, k in enumerate(("wq", "wk", "wv")):
        lc.append(pltpu.make_async_copy(r[k], r["W3"].at[i], r["ls"].at[i]))
    ta = [c.mpeer(k)[1] for k in (2, 3, 1, 0)]
    for i in range(4):
        lc.append(pltpu.make_async_copy(tok.at[ta[i]], TOK.at[ta[i]], r["ls"].at[3 + i]))
    for i in range(3):
        lc.append(pltpu.make_async_copy(wsrc[i], WA[i].at[m], r["ls"].at[7 + i]))
    for x in lc:
        x.start()
    c.barrier()

    ss, rs = r["gs"], r["gr"]
    yq = c.mpeer(2)[1]
    x0, z0 = lax.rem(c.dp, 2), lax.rem(c.dp // 2, 2)
    pc = [x0 + 2 * z0, (1 - x0) + 2 * z0, x0 + 2 * (1 - z0)]

    def rows(a, p):
        n = WA[a].shape[1] // 4
        return pl.ds(pl.multiple_of(p * n, n), n)

    yd, sd, xd, zd = c.mpeer(2), c.mpeer(1), c.dpeer(0), c.dpeer(1)
    G = {}
    for a in range(3):
        W = WA[a]
        G[a, "y"] = rcopy(wsrc[a].at[rows(a, pc[0])], W.at[m, rows(a, pc[0])], ss.at[a, 0], rs.at[a, 0], yd)
        G[a, "s"] = rcopy(wsrc[a], W.at[m], ss.at[a, 1], rs.at[a, 1], sd)

        def w(p, half=None):
            at = rows(a, p)
            if half is None:
                return W.at[yq, at]
            return W.at[yq, at, half * (d // 2) : (half + 1) * (d // 2)]

        G[a, "x"] = rcopy(w(pc[0]), w(pc[0]), ss.at[a, 2], rs.at[a, 2], xd)
        G[a, "z"] = rcopy(w(pc[0]), w(pc[0]), ss.at[a, 3], rs.at[a, 3], zd)
        G[a, "dz"] = rcopy(w(pc[1], 0), w(pc[1], 0), ss.at[a, 4], rs.at[a, 4], zd)
        G[a, "dx"] = rcopy(w(pc[2], 1), w(pc[2], 1), ss.at[a, 5], rs.at[a, 5], xd)
        G[a, "t"] = rcopy(W.at[yq], W.at[yq], ss.at[a, 6], rs.at[a, 6], sd)
    for a in range(3):
        G[a, "y"].start()
    for a in range(3):
        G[a, "s"].start()
    V = [rcopy(vec, VA.at[m], r["vs"].at[k - 1], r["vr"].at[k - 1], c.mpeer(k)) for k in (1, 2, 3)]
    for x in V:
        x.start()
    VA[m] = vec[...]

    def g_y(a):
        G[a, "y"].wait_recv()
        G[a, "x"].start()
        G[a, "z"].start()

    def g_xz(a):
        G[a, "x"].wait_recv()
        G[a, "dz"].start()
        G[a, "z"].wait_recv()
        G[a, "dx"].start()

    def g_t(a):
        G[a, "dx"].wait_recv()
        G[a, "dz"].wait_recv()
        G[a, "t"].start()

    for i in range(3):
        lc[i].wait()
        WT[i * hw : (i + 1) * hw, :] = r["W3"][i].T
    bias = vec[...].T[0 : 3 * hw, 7:8]

    sub = lax.broadcasted_iota(jnp.int32, (aug - HD, seq), 0)
    lane = lax.broadcasted_iota(jnp.int32, (aug - HD, seq), 1)
    ones = jnp.where(sub == 0, 1.0, 0.0).astype(BF)
    A = []

    def attend(s):
        t = ta[s]
        lc[3 + s].wait()
        x = TOK[t]
        qkv = (mm(WT[...], x, 1, 1) + bias).astype(BF)
        dead = jnp.where(sub == 0, jnp.where(lane < ln[t], 0.0, -1e30), 0.0).astype(BF)
        for h in range(nh):
            at = slice(h * HD, (h + 1) * HD)
            QT[t, h, 0:HD] = qkv[h * HD : (h + 1) * HD] * jnp.asarray(HD**-0.5, BF)
            QT[t, h, HD:aug] = ones
            KT[t, h, 0:HD] = qkv[hw + h * HD : hw + (h + 1) * HD]
            KT[t, h, HD:aug] = dead
        VT[t] = qkv[2 * hw : 3 * hw]
        for h in range(nh):
            at = slice(h * HD, (h + 1) * HD)
            sc = mm(KT[t, h], QT[t, h], 0, 0)
            e = jnp.exp(sc - jnp.max(sc, axis=0, keepdims=True))
            ri = 1.0 / jnp.sum(e, axis=0, keepdims=True)
            el = e.astype(BF)
            ET[t, h] = el
            RI[t, h : h + 1] = ri
            o = mm(VT[t, at], el, 1, 0) * ri
            ATQ[t, at] = o.astype(BF)
        if s < 3:
            cp = rcopy(ATQ.at[t], ATO.at[m], r["as"].at[s], r["ar"].at[s], c.mpeer((2, 3, 1)[s]))
            cp.start()
            A.append(cp)
        else:
            ATO[m] = ATQ[t]

    attend(0)
    g_y(0)
    attend(1)
    g_xz(0)
    g_y(1)
    attend(2)
    g_t(0)
    g_xz(1)
    attend(3)
    g_y(2)

    f = lambda i: vec[i : i + 1]
    WO = WA[0]
    G[0, "s"].wait_recv()
    lc[7].wait()
    for cp in A:
        cp.wait_recv()
    G[0, "t"].wait_recv()
    mixed = TOK[m].astype(F32) + f(0)
    for q in range(4):
        mixed += mm(ATO[q], WO[q], 0, 0)
    n1, i1 = norm_rows(mixed)
    N1[...] = n1
    I1[...] = i1
    first = n1 * f(1) + f(2)
    FIRST[...] = first
    FL[...] = first.astype(BF)

    for x in V:
        x.wait_recv()
    cw = d // 3

    def ffn(k):
        q = c.mpeer(k)[1]

        def chunk(j, _):
            at = pl.ds(pl.multiple_of(j * cw, 128), cw)
            h = mm(FL[...], WA[1][q, :, at], 1, 0) + VA[q, 6:7, at]
            g, gp = gelu_pair(h)
            ACT[q, :, at] = g.astype(BF)
            GP[q, :, at] = gp.astype(BF)
            return 0

        lax.fori_loop(0, 3, chunk, 0)

    def ffn2(k):
        q = c.mpeer(k)[1]
        y = mm(ACT[q], WA[2][q], 1, 0)
        if k == 0:
            ACC[...] = y
        else:
            ACC[...] += y

    lc[8].wait()
    ffn(0)
    g_t(1)
    lc[9].wait()
    ffn2(0)
    g_xz(2)
    G[1, "s"].wait_recv()
    ffn(1)
    G[2, "s"].wait_recv()
    ffn2(1)
    g_t(2)
    ffn(2)
    ffn2(2)
    G[1, "t"].wait_recv()
    ffn(3)
    G[2, "t"].wait_recv()
    ffn2(3)
    second = FIRST[...] + ACC[...] + f(3)
    n2, i2 = norm_rows(second)
    N2[...] = n2
    I2[...] = i2
    for a in range(3):
        for k in ("y", "s", "x", "z", "dz", "dx", "t"):
            G[a, k].wait_send()
    for x in V + A:
        x.wait_send()
    outs = [n for n in names if n.startswith("o_")]
    cps = [pltpu.make_async_copy(r[n[2:]], r[n], r["os"].at[i]) for i, n in enumerate(outs)]
    for x in cps:
        x.start()
    for x in cps:
        x.wait()


def forward(tok4, lengths, vec, wq, wk, wv, wo, wu, wd, nbits):
    nt, seq, d = tok4.shape
    hw = wq.shape[1]
    ff = wu.shape[1]
    nh = hw // HD
    V = pltpu.VMEM
    S = jax.ShapeDtypeStruct
    DMA = pltpu.SemaphoreType.DMA
    scratch = {
        "TOK": V((nt, seq, d), BF),
        "W3": V((3, d, hw), BF),
        "WT": V((3 * hw, d), BF),
        "QT": V((nt, nh, HD + 16, seq), BF),
        "KT": V((nt, nh, HD + 16, seq), BF),
        "VT": V((nt, hw, seq), BF),
        "ET": V((nt, nh, seq, seq), BF),
        "RI": V((nt, 8, seq), F32),
        "ATQ": V((nt, hw, seq), BF),
        "ATO": V((nt, hw, seq), BF),
        "N1": V((seq, d), F32),
        "I1": V((seq, 1), F32),
        "FIRST": V((seq, d), F32),
        "FL": V((seq, d), BF),
        "ACT": V((nt, seq, ff), BF),
        "GP": V((nt, seq, ff), BF),
        "WOA": V((nt, hw, d), BF),
        "UA": V((nt, d, ff), BF),
        "DA": V((nt, ff, d), BF),
        "VA": V((nt, 8, d), F32),
        "ACC": V((seq, d), F32),
        "N2": V((seq, d), F32),
        "I2": V((seq, 1), F32),
        "ls": DMA((10,)),
        "gs": DMA((3, 7)),
        "gr": DMA((3, 7)),
        "vs": DMA((3,)),
        "vr": DMA((3,)),
        "as": DMA((3,)),
        "ar": DMA((3,)),
        "os": DMA((24,)),
    }
    ins = {"len": lengths, "vec": vec, "tok": tok4, "wq": wq, "wk": wk, "wv": wv, "wo": wo, "wu": wu, "wd": wd}
    specs = [pl.BlockSpec(memory_space=pltpu.SMEM), pl.BlockSpec(memory_space=V)]
    specs += [pl.BlockSpec(memory_space=pl.ANY)] * (len(ins) - 2)
    outs = [
        "QT", "KT", "VT", "ET", "RI", "ATQ", "ATO", "N1", "I1", "FL", "ACT", "GP", "WOA", "UA", "DA", "N2", "I2",
    ]
    names = list(ins) + ["o_" + n for n in outs] + list(scratch)
    res = pl.pallas_call(
        functools.partial(fwd_kernel, nbits, names),
        out_shape=[S(scratch[n].shape, scratch[n].dtype) for n in outs],
        in_specs=specs,
        out_specs=[pl.BlockSpec(memory_space=pl.ANY)] * len(outs),
        scratch_shapes=list(scratch.values()),
        compiler_params=pltpu.CompilerParams(
            collective_id=0, has_side_effects=True, vmem_limit_bytes=60 * 2**20
        ),
    )(*ins.values())
    return dict(zip(outs, res))


def norm_back(up, normed, inv, gain):
    c = up * gain
    return inv * (
        c
        - jnp.mean(c, axis=-1, keepdims=True)
        - normed * jnp.mean(c * normed, axis=-1, keepdims=True)
    )


def shards(
    tokens, lengths, wq, bq, wk, wv, bv, wo, bo, g1, s1, wu, bu, wd, bd, g2, s2, cot
):
    n = lengths.shape[0]
    rows, d = tokens.shape
    seq = rows // n
    hw = wq.shape[1]
    m = lax.axis_index("mp")
    nd = lax.axis_size("dp")
    own = lambda a: lax.dynamic_slice_in_dim(a, m * seq, seq, 0)
    f = lambda a: a.astype(F32)
    zero = jnp.zeros((hw,), F32)
    vec = jnp.stack(
        [f(a) for a in (bo, g1, s1, bd, g2, s2, bu)] + [jnp.concatenate([f(bq), zero, f(bv), zero])]
    )
    tok4 = tokens.reshape(n, seq, d)
    F = forward(tok4, lengths, vec, wq, wk, wv, wo, wu, wd, nd.bit_length() - 1)
    n1, i1, n2, i2, first_low = F["N1"], F["I1"], F["N2"], F["I2"], F["FL"]
    att_own, act, gp = F["ATO"], F["ACT"], F["GP"]
    out_own = (n2 * f(g2) + f(s2)).astype(BF)
    c_own = f(own(cot))
    d2 = norm_back(c_own, n2, i2, f(g2))
    d2l = d2.astype(BF)
    dg2, ds2, dbd = jnp.sum(c_own * n2, 0), jnp.sum(c_own, 0), jnp.sum(d2, 0)
    dwd = jnp.einsum("qtf,td->qfd", act, d2l, preferred_element_type=F32)
    dact = jnp.einsum("td,qfd->qtf", d2l, F["DA"], preferred_element_type=F32)
    dh = (dact * f(gp)).astype(BF)
    dbu = jnp.sum(f(dh), axis=1)
    dwu = jnp.einsum("td,qtf->qdf", first_low, dh, preferred_element_type=F32)
    d1 = d2 + jnp.einsum("qtf,qdf->td", dh, F["UA"], preferred_element_type=F32)
    dg1, ds1 = jnp.sum(d1 * n1, 0), jnp.sum(d1, 0)
    dm = norm_back(d1, n1, i1, f(g1))
    dbo = jnp.sum(dm, 0)
    dml = dm.astype(BF)
    dwo = jnp.einsum("qkt,td->qkd", att_own, dml, preferred_element_type=F32)
    datt = jnp.einsum("td,qkd->qkt", dml, F["WOA"], preferred_element_type=F32).astype(BF)
    datt = lax.all_to_all(datt, "mp", 0, 0)
    hs = (n, hw // HD, HD, seq)
    doh = f(datt).reshape(hs) * F["RI"][:, : hw // HD, None, :]
    dd = jnp.sum(doh * f(F["ATQ"]).reshape(hs), axis=2, keepdims=True)
    dol = doh.astype(BF)
    e = F["ET"]
    q, k, v = F["QT"][:, :, :HD], F["KT"][:, :, :HD], F["VT"].reshape(hs)
    es = functools.partial(jnp.einsum, preferred_element_type=F32)
    dv = es("thkq,thdq->thdk", e, dol)
    dp = es("thdk,thdq->thkq", v, dol)
    ds = (f(e) * (dp - dd)).astype(BF)
    dq = es("thkq,thdk->thdq", ds, k) * HD**-0.5
    dk = es("thkq,thdq->thdk", ds, q)
    dq, dk, dv = (a.reshape(n, hw, seq).astype(BF) for a in (dq, dk, dv))
    dbq, dbv = jnp.sum(f(dq), (0, 2)), jnp.sum(f(dv), (0, 2))
    dwq, dwk, dwv = (es("tsd,tws->dw", tok4, a) for a in (dq, dk, dv))
    back = (es("tws,dw->tsd", dq, wq) + es("tws,dw->tsd", dk, wk) + es("tws,dw->tsd", dv, wv)).astype(BF)
    back = jnp.sum(f(lax.all_to_all(back, "mp", 0, 0)), 0)
    tg_own = (dm + back).astype(BF)
    layer_out = lax.all_gather(out_own, "mp", tiled=True)
    tokens_grad = lax.all_gather(tg_own, "mp", tiled=True)
    low = lambda a: a.astype(BF)
    ffn = lax.psum_scatter(jnp.stack([low(dwu), low(dwd)], 1), "mp", scatter_dimension=0)
    dwo = lax.psum_scatter(low(dwo), "mp", scatter_dimension=0)
    dbu = lax.psum_scatter(dbu, "mp", scatter_dimension=0)
    dwq, dwk, dwv, dwo, ffn = lax.psum((low(dwq), low(dwk), low(dwv), dwo, ffn), "dp")
    dbq, dbv, dbu = lax.psum((dbq, dbv, dbu), "dp")
    dbo, dg1, ds1, dbd, dg2, ds2 = lax.psum((dbo, dg1, ds1, dbd, dg2, ds2), ("dp", "mp"))
    return (
        layer_out, tokens_grad, f(dwq), dbq, f(dwk), f(dwv), dbv, f(dwo), dbo, dg1, ds1,
        f(ffn[0]), dbu, f(ffn[1]), dbd, dg2, ds2,
    )


def solution(mesh):
    row, col, one, rep = P("dp", None), P(None, "mp"), P("mp"), P()
    low = P("mp", None)
    in_specs = (
        row, P("dp"), col, one, col, col, one, low, rep, rep, rep, col, one, low, rep, rep, rep, row,
    )
    out_specs = (
        row, row, col, one, col, col, one, low, rep, rep, rep, col, one, low, rep, rep, rep,
    )
    return jax.shard_map(shards, mesh=mesh, in_specs=in_specs, out_specs=out_specs, check_vma=False)
```

time: 625 us -> 591 us (0.946)
  Pallas kernels: 0 us -> 58 us
  matrix products: 88.1 us -> 41.1 us
  local copies, waits for them, and re-layouts: 76 us -> 31.5 us
  waiting for transfers between devices: 235 us -> 258 us
  blocking collectives: 166 us -> 147 us
    pallas_call x0 -> x1, Pallas kernels: none -> 58 us  [forward(): pl.pallas_call(functools.partial(fwd_kernel, nbits, names), out_shape=[S(...]
    dot_general x40 -> x14, matrix products: 79.1 us -> 32.4 us  [the longest x3 6.53 us: shards(): dwq, dwk, dwv = (es('tsd,tws->dw', tok4, a) for a in (dq, dk, dv))]
    unnamed x9 -> x6, waiting for transfers between devices: 38.3 us -> 78.6 us
    dynamic_slice x40 -> x0, local copies, waits for them, and re-layouts: 38.8 us -> none  [the longest x32 29.8 us: shards(): lax.map(attend_forward, (by_table(q), by_table(k), by_table(v), lengths))]
    all_gather x1 -> x0, blocking collectives: 22.1 us -> none  [shards(): bu_all = lax.all_gather(f(bu), 'mp')]
    all_gather x3 -> x0, waiting for transfers between devices: 17.8 us -> none  [the longest x1 17.8 us: shards(): wd_all = lax.all_gather(wd, 'mp')]
    dynamic_update_slice x12 -> x0, local copies, waits for them, and re-layouts: 8.77 us -> none  [shards(): lax.map(attend_forward, (by_table(q), by_table(k), by_table(v), lengths))]
    dynamic_update_slice x8 -> x0, other arithmetic: 6.97 us -> none  [shards(): lax.map(attend_forward, (by_table(q), by_table(k), by_table(v), lengths))]
  transfers between devices with their start and end apart: 10 -> 6, of which waited for: 5 -> 4; matrix products, arithmetic and copies ran while one was open for 23% -> 7% of each run, Pallas kernels for 0% -> 0%
where the time goes in v2:
time: 591 us; the launch traced here: 583 us
  waiting for transfers between devices  258 us (44%)
  blocking collectives  147 us (25%)
  Pallas kernels  58 us (10%)
  matrix products  41.1 us (7%)
  local copies, waits for them, and re-layouts  31.5 us (5%)
  other arithmetic  28.9 us (5%)
  between operations  14.7 us (2%)
    psum x1, waiting for transfers between devices, shards(): lax.psum((low(dwq), low(dwk), low(dwv), dwo, ffn), 'dp')  135 us
    unnamed x6, waiting for transfers between devices  78.6 us
    all_to_all x1, blocking collectives, shards(): back = jnp.sum(f(lax.all_to_all(back, 'mp', 0, 0)), 0)  73 us
    pallas_call x1, Pallas kernels, forward(): pl.pallas_call(functools.partial(fwd_kernel, nbits, names), out_shape=[S(...  58 us
    psum x1, blocking collectives, shards(): lax.psum((dbo, dg1, ds1, dbd, dg2, ds2), ('dp', 'mp'))  41.6 us
    reduce_scatter x1, waiting for transfers between devices, shards(): dwo = lax.psum_scatter(low(dwo), 'mp', scatter_dimension=0)  25.2 us
    psum x1, blocking collectives, shards(): dbq, dbv, dbu = lax.psum((dbq, dbv, dbu), 'dp')  21.8 us
    unnamed x72, local copies, waits for them, and re-layouts  21.3 us
  transfers between devices with their start and end apart: 6, of which 4 were waited for; matrix products, arithmetic and copies ran while one was open for 7% of the time, Pallas kernels for 0%

profile of v2, /device:TPU:0, one launch (start us, length us, event | category | flops | bytes accessed | tf_op | source)
XLA Modules:
  0.0 583.2 jit_solution(5242404445596542836)
XLA Ops:
  21.1 58.0 %shard_map.305 = (bf16[4,3,80,512]{3,2,1,0:T(8,128)(2,1)}, bf16[4,3,80,512]{3,2,1,0:T(8,128)(2,1)}, bf16[4,192,512]{2,1,0:T(8,128)(2,1)}, bf16[4,3,512,512]{3,2,...) custom-call(s32[4]{0:T(128)} %refs_0_.1, ...), custom_call_target="tpu_custom_call" | custom-call | tf_op jit(solution)/shard_map/pallas_call | solution.py:327
  80.3 2.3 fusion.7
  82.6 2.7 fusion.36
  85.3 4.4 convert_bitcast_fusion
  89.7 2.9 convert_reduce_fusion
  94.3 4.3 convert_bitcast_fusion.1
  98.6 8.3 %pad_maximum_fusion = bf16[4,2,768,768]{2,3,0,1:T(8,128)(2,1)} fusion(bf16[4,1,768,768]{2,3,0,1:T(8,128)(2,1)} %convert_bitcast_fusion, bf16[4,1,768,768]{2,3,0,1:T(8,128)(2,1)} %convert_bitcast_fusion.1), kind=kLoop, calls=%fused_computation.1 | loop fusion | flops 4718592 | bytes 18874368 | tf_op jit(solution)/shard_map/stack | solution.py:407
  108.8 6.2 %multiply_reduce_fusion = (f32[768]{0:T(1024)S(1)}, f32[512]{0:T(512)S(1)}, f32[512]{0:T(512)S(1)}, f32[768]{0:T(1024)S(1)}, f32[512,768]{1,0:T(8,128)S(1)}) fusion(f32[512,768]{1,0:T(8,128)S(1)} %copy-done.9, f32[768]{0:T(1024)S(1)} %convert_element_type.149, f32[512,768]{1,0:T(8,128)S(1)} %copy-done.11, bf16[4,512,768]{2,1,0:T(8,128)(2,1)} %copy-done.27, ...), kind=kOutput, calls=%fused_computation.25 | convolution fusion | flops 2419062272 | bytes 12596224 | tf_op jit(solution)/shard_map/qtf,qdf->td/dot_general | solution.py:378
  119.8 3.6 all-to-all-start
  124.2 19.6 %all-to-all-done = bf16[4,192,512]{2,1,0:T(8,128)(2,1)S(1)} async-done(((bf16[4,192,512]{2,1,0:T(8,128)(2,1)}), bf16[4,192,512]{2,1,0:T(8,128)(2,1)S(1)}, u32[]{:S(2)}, u32[]{:S(2)}) %all-to-all-start) | async-done | bytes 786464 | tf_op jit(solution)/shard_map/all_to_all | solution.py:385
  145.3 4.8 multiply_convert_fusion
  150.1 2.0 convolution_convert_fusion.3
  156.0 2.1 convert_reduce_fusion.3
  159.2 73.0 %all_to_all.10 = bf16[4,512,768]{2,1,0:T(8,128)(2,1)S(1)} all-to-all(bf16[4,512,768]{2,1,0:T(8,128)(2,1)S(1)} %add_convert_fusion), channel_id=1, replica_groups=mesh['dp'=8,'mp'=4] {'mp'}, dimensions={0} | all-to-all | bytes 6291456 | tf_op jit(solution)/shard_map/all_to_all | solution.py:402
  234.5 3.5 fusion.15
  241.0 77.8 %all-reduce.8.cloned.1.call-done = bf16[4,2,768,768]{2,3,0,1:T(8,128)(2,1)} async-done(((bf16[4,2,768,768]{2,3,0,1:T(8,128)(2,1)}), bf16[4,2,768,768]{2,3,0,1:T(8,128)(2,1)}) %all-reduce.8.cloned.1.call-update) | async-done | bytes 9437200
  318.8 3.9 dynamic-slice_bitcast_fusion
  322.7 25.2 %reduce-scatter.5.cloned.1.call-done = bf16[1,192,768]{2,1,0:T(8,128)(2,1)} async-done(((bf16[4,192,768]{2,1,0:T(8,128)(2,1)}), bf16[1,192,768]{2,1,0:T(8,128)(2,1)}) %reduce-scatter.5.cloned.1.call-update) | async-done | bytes 294928 | tf_op jit(solution)/shard_map/reduce_scatter | solution.py:408
  347.9 10.1 %all-reduce.1 = f32[4,768]{1,0:T(4,128)S(1)} all-reduce(f32[4,768]{1,0:T(4,128)S(1)} %get-tuple-element.136), channel_id=4, replica_groups=mesh['dp'=8,'mp'=4] {'mp'}, use_global_device_ids=true, to_apply=%region_24.0.clone | all-reduce | flops 3072 | bytes 24576
  358.7 41.6 %all-reduce.2 = (f32[768]{0:T(1024)}, f32[768]{0:T(1024)}, f32[768]{0:T(1024)}, f32[768]{0:T(1024)}, f32[768]{0:T(1024)}, /*index=5*/f32[768]{0:T(1024)}) all-reduce(f32[768]{0:T(1024)S(1)} %get-tuple-element.126, f32[768]{0:T(1024)S(1)} %get-tuple-element.106, ...), channel_id=1, replica_groups=mesh['dp'=8,'mp'=4] {'dp','mp'}, use_global_device_ids=true, to_apply=%region_16.0 | all-reduce | flops 4608 | bytes 36864 | tf_op jit(solution)/shard_map/psum | solution.py:412
  400.4 21.8 %all-reduce.3 = (f32[192]{0:T(256)}, f32[192]{0:T(256)}, f32[768]{0:T(1024)}) all-reduce(f32[192]{0:T(256)S(1)} %reduce_sum.146, f32[192]{0:T(256)S(1)} %reduce_sum.148, f32[768]{0:T(1024)S(1)} %dynamic-slice_reduce_fusion), channel_id=1, replica_groups=mesh['dp'=8,'mp'=4] {'dp'}, use_global_device_ids=true, to_apply=%region_8.0 | all-reduce | flops 1152 | bytes 9216 | tf_op jit(solution)/shard_map/psum | solution.py:411
  422.3 135.1 %all-reduce.10.cloned.1.call-done = (bf16[768,192]{0,1:T(8,128)(2,1)}, bf16[768,192]{0,1:T(8,128)(2,1)}, bf16[768,192]{0,1:T(8,128)(2,1)}, bf16[192,768]{1,0:T(8,128)(2,1)}, bf16[2,768,768]{1,2,0:T(8,128)(2,1)}) async-done(((bf16[768,192]{0,1:T(8,128)(2,1)}, bf16[768,192]{0,1:T(8,128)(2,1)}, bf16[768,192]{0,1:T(8,128)(2,1)}, bf16[192,768]{1,0:T(8,128)(2,1)}, bf16[2,768,768]{1,2,0:T(8,128)(2,1)}), ...) | async-done | bytes 3538960 | tf_op jit(solution)/shard_map/psum | solution.py:410
  565.6 3.0 copy.58
  570.6 3.9 copy.72
  (126 shorter events, 48.3 us)
Async XLA Ops:
  7.2 311.6 %all-reduce.8.cloned.1.call-start = ((), (), s32[]{:S(2)}) async-start(), calls=%async_computation.6 | async-start | bytes 18874368
  79.1 3.6 copy-start
  80.3 5.0 copy-start.23
  82.6 7.1 %slice-start.2 = ((s8[4718592]{0:T(1024)(128)(4,1)}), s8[4194304]{0:T(1024)(128)(4,1)S(1)}, s32[]{:S(2)}) async-start(s8[4718592]{0:T(1024)(128)(4,1)} %bitcast.129), calls=%async_computation.10 | async-start | bytes 8388608
  85.3 4.4 copy-start.10
  85.3 4.4 slice-start.3
  85.3 4.4 copy-start.22
  89.7 4.6 copy-start.25
  106.9 241.0 %reduce-scatter.5.cloned.1.call-start = ((), (), s32[]{:S(2)}) async-start(), calls=%async_computation.5 | async-start | bytes 1474560 | tf_op jit(solution)/shard_map/reduce_scatter | solution.py:408
  118.1 6.1 %copy-start.20 = (f32[4,8,512]{2,1,0:T(8,128)S(1)}, f32[4,8,512]{2,1,0:T(8,128)}, u32[]{:S(2)}) copy-start(f32[4,8,512]{2,1,0:T(8,128)} %get-tuple-element.45) | copy-start | bytes 196612
  119.8 25.5 %copy-start.8 = (bf16[4,192,512]{2,1,0:T(8,128)(2,1)S(1)}, bf16[4,192,512]{2,1,0:T(8,128)(2,1)}, u32[]{:S(2)}) copy-start(bf16[4,192,512]{2,1,0:T(8,128)(2,1)} %get-tuple-element.43) | copy-start | bytes 2359300
  119.8 24.0 %all-to-all-start = ((bf16[4,192,512]{2,1,0:T(8,128)(2,1)}), bf16[4,192,512]{2,1,0:T(8,128)(2,1)S(1)}, u32[]{:S(2)}, u32[]{:S(2)}) async-start(bf16[4,192,512]{2,1,0:T(8,128)(2,1)} %convolution_convert_fusion.1), calls=%async_computation | async-start | bytes 1572864 | tf_op jit(solution)/shard_map/all_to_all | solution.py:385
  123.4 298.9 %all-gather.3.cloned.1.call-start = ((), (), s32[]{:S(2)}) async-start(), calls=%async_computation.3 | async-start | bytes 3932160 | tf_op jit(solution)/shard_map/all_gather | solution.py:404
  124.2 298.1 %all-gather.5.cloned.1.call-start = ((), (), s32[]{:S(2)}) async-start(), calls=%async_computation.4 | async-start | bytes 3932160 | tf_op jit(solution)/shard_map/all_gather | solution.py:405
  145.2 4.9 copy-start.12
  152.1 3.8 slice-start
  153.4 2.6 slice-start.1
  156.0 2.1 copy-start.15
  233.8 323.6 %all-reduce.10.cloned.1.call-start = ((), (), s32[]{:S(2)}) async-start(), calls=%async_computation.7 | async-start | bytes 7077888 | tf_op jit(solution)/shard_map/psum | solution.py:410
  234.4 3.5 copy-start.4
  234.4 3.5 copy-start.5
  557.4 5.6 copy-start.18
  557.4 6.5 %copy-start.7 = (bf16[2,768,768]{1,2,0:T(8,128)(2,1)S(1)}, bf16[2,768,768]{1,2,0:T(8,128)(2,1)}, u32[]{:S(2)}) copy-start(bf16[2,768,768]{1,2,0:T(8,128)(2,1)} %get-tuple-element.123) | copy-start | bytes 7077892
  570.6 3.9 copy-start.6
  (14 other events, 19.7 us)
Sparse Core Ops, SparseCore 0:
  107.0 211.7 all-reduce.7
  321.9 25.8 reduce-scatter.4
  350.1 29.2 all-gather.2
  381.4 29.1 all-gather.4
  416.3 141.0 all-reduce.9

commit v3 on v2

--- a/solution.py
+++ b/solution.py
@@ -35,6 +35,18 @@
     return h * phi, phi + h * e * 0.3989422804014327
 
 
+def add_rows(dst, src, n):
+    step = 48
+
+    def body(i, _):
+        at = pl.ds(pl.multiple_of(i * step, 16), step)
+        a, b = dst.at[at], src.at[at]
+        a[...] = (a[...].astype(F32) + b[...].astype(F32)).astype(BF)
+        return 0
+
+    lax.fori_loop(0, n // step, body, 0)
+
+
 def norm_rows(x):
     center = x - jnp.mean(x, axis=-1, keepdims=True)
     inv = lax.rsqrt(jnp.mean(center * center, axis=-1, keepdims=True) + EPS)
@@ -70,13 +82,114 @@
     )
 
 
-def fwd_kernel(nbits, names, *refs):
+class Unit:
+    def __init__(self, c, view, rows, order, slots, ss, rs, out, loc):
+        self.stages = []
+        self.sent = []
+        y = c.mp // 2
+        hs = [0, 1] if "y" in order else [0]
+        own = 0
+        off, n = 0, rows
+        pend = []
+        k = 0
+        spans = []
+
+        def put(a, b, dev):
+            nonlocal k
+            cp = rcopy(a, b, ss.at[k], rs.at[k], dev)
+            k += 1
+            return cp
+
+        steps = []
+        for i, ax in enumerate(order):
+            if ax == "y":
+                cps = [put(view(1 - y, off, n), slots[i].at[0], c.mpeer(2))]
+                hs, own = [y], y
+                adds = [(view(y, off, n), slots[i].at[0], n)]
+            else:
+                b = "xz".index(ax)
+                bit = lax.rem(c.dp // (1 << b), 2)
+                spans.append((b, off, n))
+                n //= 2
+                mine, theirs = off + bit * n, off + (1 - bit) * n
+                cps, adds = [], []
+                for j, h in enumerate(hs):
+                    cps.append(put(view(h, theirs, n), slots[i].at[j], c.dpeer(b)))
+                    adds.append((view(h, mine, n), slots[i].at[j], n))
+                off = mine
+            steps.append((cps, adds, False))
+        for b in range(2, c.nbits):
+            sl = slots[len(order) + b - 2]
+            steps.append(([put(view(own, off, n), sl.at[0], c.dpeer(b))], [(view(own, off, n), sl.at[0], n)], True))
+        (b2, _, _), (b1, o1, _) = spans
+        mine = view(own, off, n)
+        bit = lax.rem(c.dp // (1 << b1), 2)
+        theirs = o1 + (1 - bit) * n
+        first = put(mine, out(off, n), c.dpeer(b1))
+        second = put(mine, out(off, n), c.dpeer(b2))
+        third = put(out(theirs, n), out(theirs, n), c.dpeer(b2))
+        self.local = pltpu.make_async_copy(mine, out(off, n), loc)
+        steps.append(([first, second], [], False))
+        steps.append(([third], [], False))
+        self.steps = steps
+        self.at = 0
+        self.hold = second
+
+    def go(self):
+        last = len(self.steps)
+        if self.at > 0:
+            cps, adds, both = self.steps[self.at - 1]
+            for cp in cps:
+                if cp is not self.hold:
+                    cp.wait_recv()
+                if both:
+                    cp.wait_send()
+                else:
+                    self.sent.append(cp)
+            for a in adds:
+                add_rows(*a)
+        if self.at < last:
+            for cp in self.steps[self.at][0]:
+                cp.start()
+            if self.at == last - 2:
+                self.local.start()
+        else:
+            self.hold.wait_recv()
+        self.at += 1
+
+    def drain(self):
+        for cp in self.sent:
+            cp.wait_send()
+        self.local.wait()
+
+
+class Swap:
+    def __init__(self, ref, slots, ss, rs, peers):
+        self.ref, self.slots = ref, slots
+        self.cps = [rcopy(ref, slots.at[i], ss.at[i], rs.at[i], p) for i, p in enumerate(peers)]
+        self.at = 0
+
+    def go(self):
+        if self.at > 0:
+            self.cps[self.at - 1].wait()
+            self.ref[...] += self.slots[self.at - 1]
+        if self.at < len(self.cps):
+            self.cps[self.at].start()
+        self.at += 1
+
+    def end(self):
+        while self.at <= len(self.cps):
+            self.go()
+
+
+def layer_kernel(nbits, names, *refs):
     r = dict(zip(names, refs))
     ln, vec, tok = r["len"], r["vec"], r["tok"]
     TOK, WT, QT, KT, VT, ET, RI = (r[k] for k in ("TOK", "WT", "QT", "KT", "VT", "ET", "RI"))
     ATQ, ATO, N1, I1, FL, ACT, GP = (r[k] for k in ("ATQ", "ATO", "N1", "I1", "FL", "ACT", "GP"))
     WA = (r["WOA"], r["UA"], r["DA"])
-    VA, FIRST, ACC, N2, I2 = (r[k] for k in ("VA", "FIRST", "ACC", "N2", "I2"))
+    VA, ACC, COT, SA, SFL, SAT = (r[k] for k in ("VA", "ACC", "COT", "SA", "SFL", "SAT"))
+    D2L, SD2, SH, DOT, DTS, SG, BQ = (r[k] for k in ("D2L", "SD2", "SH", "DOT", "DTS", "SG", "BQ"))
     wsrc = (r["wo"], r["wu"], r["wd"])
     c = Comm(nbits)
     m = c.mp
@@ -93,9 +206,16 @@
         lc.append(pltpu.make_async_copy(tok.at[ta[i]], TOK.at[ta[i]], r["ls"].at[3 + i]))
     for i in range(3):
         lc.append(pltpu.make_async_copy(wsrc[i], WA[i].at[m], r["ls"].at[7 + i]))
+    lc.append(pltpu.make_async_copy(r["cot"].at[m], COT, r["ls"].at[10]))
     for x in lc:
         x.start()
     c.barrier()
+    cb, yb = lax.rem(m, 2), m // 2
+    sd = c.mpeer(1)
+    C = [rcopy(ATO.at[1 - cb + 2 * h], SAT.at[h], r["cs"].at[h], r["cr"].at[h], sd) for h in (0, 1)]
+    C.append(rcopy(FL, SFL, r["cs"].at[2], r["cr"].at[2], sd))
+    for i, h in enumerate((yb, 1 - yb)):
+        C.append(rcopy(ACT.at[1 - cb + 2 * h], SA.at[h], r["cs"].at[3 + i], r["cr"].at[3 + i], sd))
 
     ss, rs = r["gs"], r["gr"]
     yq = c.mpeer(2)[1]
@@ -210,12 +330,21 @@
     mixed = TOK[m].astype(F32) + f(0)
     for q in range(4):
         mixed += mm(ATO[q], WO[q], 0, 0)
-    n1, i1 = norm_rows(mixed)
-    N1[...] = n1
-    I1[...] = i1
-    first = n1 * f(1) + f(2)
-    FIRST[...] = first
-    FL[...] = first.astype(BF)
+    ACC[...] = mixed
+    C[0].start()
+    C[1].start()
+    nr = 64
+
+    def norm1(i, _):
+        at = pl.ds(pl.multiple_of(i * nr, nr), nr)
+        n1, i1 = norm_rows(ACC[at])
+        N1[at] = n1
+        I1[at] = i1
+        FL[at] = (n1 * f(1) + f(2)).astype(BF)
+        return 0
+
+    lax.fori_loop(0, seq // nr, norm1, 0)
+    C[2].start()
 
     for x in V:
         x.wait_recv()
@@ -250,6 +379,7 @@
     g_xz(2)
     G[1, "s"].wait_recv()
     ffn(1)
+    C[3].start()
     G[2, "s"].wait_recv()
     ffn2(1)
     g_t(2)
@@ -257,26 +387,320 @@
     ffn2(2)
     G[1, "t"].wait_recv()
     ffn(3)
+    C[4].start()
     G[2, "t"].wait_recv()
     ffn2(3)
-    second = FIRST[...] + ACC[...] + f(3)
-    n2, i2 = norm_rows(second)
-    N2[...] = n2
-    I2[...] = i2
+    lc[10].wait()
+
+    def fold(x):
+        return jnp.sum(x.reshape(x.shape[0] // 8, 8, x.shape[1]), axis=0)
+
+    zero = jnp.zeros((8, d), F32)
+
+    def norm2(i, sums):
+        at = pl.ds(pl.multiple_of(i * nr, nr), nr)
+        n2, i2 = norm_rows(N1[at] * f(1) + f(2) + ACC[at] + f(3))
+        ct = COT[at].astype(F32)
+        COT[at] = (n2 * f(4) + f(5)).astype(BF)
+        cg = ct * f(4)
+        cn = ct * n2
+        d2 = i2 * (
+            cg
+            - jnp.mean(cg, axis=-1, keepdims=True)
+            - n2 * jnp.mean(cg * n2, axis=-1, keepdims=True)
+        )
+        ACC[at] = d2
+        D2L[at] = d2.astype(BF)
+        return sums[0] + fold(d2), sums[1] + fold(cn), sums[2] + fold(ct)
+
+    sums = lax.fori_loop(0, seq // nr, norm2, (zero,) * 3)
+    SG[...] = jnp.zeros(SG.shape, F32)
+    for i in range(3):
+        SG[3 + i : 4 + i] = jnp.sum(sums[i], axis=0, keepdims=True)
+    yd = c.mpeer(2)
+    bs, br = r["bs"], r["br"]
+    E = [rcopy(D2L, SD2, bs.at[0], br.at[0], sd)]
+    E[0].start()
+    LO, TG, LOB = r["o_LO"], r["o_TG"], COT
+
+    def spread(OUT, base):
+        loc = pltpu.make_async_copy(LOB, OUT.at[m], r["os"].at[base // 3])
+        y = rcopy(LOB, OUT.at[m], r["ps"].at[base], r["pr"].at[base], yd)
+        s = rcopy(LOB, OUT.at[m], r["ps"].at[base + 1], r["pr"].at[base + 1], sd)
+        t = rcopy(OUT.at[yq], OUT.at[yq], r["ps"].at[base + 2], r["pr"].at[base + 2], sd)
+        y.start()
+        s.start()
+        loc.start()
+        return loc, y, s, t
+
+    L = spread(LO, 0)
+
+    def d_hidden(k):
+        q = c.mpeer(k)[1]
+
+        def chunk(j, _):
+            at = pl.ds(pl.multiple_of(j * cw, 128), cw)
+            dh = (mm(D2L[...], DA[q, at, :], 1, 1) * GP[q, :, at].astype(F32)).astype(BF)
+            GP[q, :, at] = dh
+            SG[pl.ds(8 + q, 1), at] = jnp.sum(dh.astype(F32), axis=0, keepdims=True)
+            return 0
+
+        lax.fori_loop(0, 3, chunk, 0)
+        if k in (1, 3):
+            h = yb if k == 1 else 1 - yb
+            cp = rcopy(GP.at[q], SH.at[h], bs.at[1 + k // 2], br.at[1 + k // 2], sd)
+            cp.start()
+            E.append(cp)
+
+    UA, DA = WA[1], WA[2]
+    GD, GU, GO = r["GD"], r["GU"], r["GO"]
+    half = d // 2
+
+    def weight_grad(G, left, right, sleft, sright, i):
+        at = slice(i * half, (i + 1) * half)
+
+        def body(h, _):
+            q = cb + 2 * h
+            G[h, at] = (left(q, h, at, right) + sleft(q, h, at, sright)).astype(BF)
+            return 0
+
+        lax.fori_loop(0, 2, body, 0)
+
+    def view(G, base):
+        def at(h, off, n):
+            if isinstance(off, int):
+                return G.at[h, base + off : base + off + n]
+            return G.at[h, pl.ds(pl.multiple_of(base + off, 16), n)]
+
+        return at
+
+    us, ur = r["us"], r["ur"]
+    nex = nbits - 2
+
+    def rows_of(O, base):
+        def at(off, n):
+            return O.at[pl.ds(pl.multiple_of(base + off, 16), n)]
+
+        return at
+
+    def unit(j, G, base, rows, order, slots, out, at):
+        return Unit(
+            c, view(G, base), rows, order, slots, us.at[j], ur.at[j], rows_of(out, at), r["os"].at[2 + j]
+        )
+
+    def ffn_slots(j, order):
+        n = half
+        h = 2
+        res = []
+        for i, ax in enumerate(order):
+            if ax == "y":
+                h = 1
+            else:
+                n //= 2
+            res.append(r["R%d%d" % (j, i)])
+        return res + [r["X%d" % j].at[e] for e in range(nex)]
+
+    orders = ORDERS
+    d_hidden(1)
+    E[0].wait_recv()
+    C[3].wait_recv()
+    C[4].wait_recv()
+    U = []
+    for i in range(2):
+        weight_grad(
+            GD,
+            lambda q, h, at, _: mm(ACT[q, :, at], D2L[...], 0, 0), None,
+            lambda q, h, at, _: mm(SA[h, :, at], SD2[...], 0, 0), None, i,
+        )
+        U.append(unit(i, GD, i * half, half, orders[i], ffn_slots(i, orders[i]), r["o_OD"], i * half))
+        U[-1].go()
+    d_hidden(3)
+    d_hidden(0)
+    d_hidden(2)
+    for x in E[1:]:
+        x.wait_recv()
+    C[2].wait_recv()
+    for i in range(2):
+        weight_grad(
+            GU,
+            lambda q, h, at, _: mm(FL[:, at], GP[q], 0, 0), None,
+            lambda q, h, at, _: mm(SFL[:, at], SH[h], 0, 0), None, i,
+        )
+        U.append(unit(2 + i, GU, i * half, half, orders[2 + i], ffn_slots(2 + i, orders[2 + i]), r["o_OU"], i * half))
+        U[-1].go()
+
+    def d_first(q, _):
+        ACC[...] += mm(GP[q], UA[q], 1, 1)
+        return 0
+
+    lax.fori_loop(0, 4, d_first, 0)
+    for x in E + C[3:5]:
+        x.wait_send()
     for a in range(3):
         for k in ("y", "s", "x", "z", "dz", "dx", "t"):
             G[a, k].wait_send()
-    for x in V + A:
+    DML = D2L
+
+    def norm1_back(i, sums):
+        at = pl.ds(pl.multiple_of(i * nr, nr), nr)
+        d1, n1 = ACC[at], N1[at]
+        cg = d1 * f(1)
+        dm = I1[at] * (
+            cg
+            - jnp.mean(cg, axis=-1, keepdims=True)
+            - n1 * jnp.mean(cg * n1, axis=-1, keepdims=True)
+        )
+        ACC[at] = dm
+        DML[at] = dm.astype(BF)
+        return sums[0] + fold(dm), sums[1] + fold(d1 * n1), sums[2] + fold(d1)
+
+    sums = lax.fori_loop(0, seq // nr, norm1_back, (zero,) * 3)
+    for i in range(3):
+        SG[i : 1 + i] = jnp.sum(sums[i], axis=0, keepdims=True)
+    M = rcopy(DML, SD2, bs.at[3], br.at[3], sd)
+    M.start()
+    dps = [c.dpeer(b) for b in range(nbits)]
+    S = Swap(SG, r["SGR"], r["ws"], r["wr"], [sd, yd] + dps)
+    S.go()
+    H = {}
+    for k in (2, 3, 1, 0):
+        q = c.mpeer(k)[1]
+        g = mm(WO[q], DML[...], 1, 1).astype(BF)
+        if k == 0:
+            DOT[m] = g
+        else:
+            DTS[q] = g
+            H[k] = rcopy(DTS.at[q], DOT.at[m], r["hs"].at[k - 1], r["hr"].at[k - 1], c.mpeer(k))
+            H[k].start()
+    M.wait_recv()
+    C[0].wait_recv()
+    C[1].wait_recv()
+    for h in (0, 1):
+        q = cb + 2 * h
+        GO[h] = (mm(ATO[q], DML[...], 1, 0) + mm(SAT[h], SD2[...], 1, 0)).astype(BF)
+    oslots = [r["R40"], r["R41"], r["R42"]] + [r["X4"].at[e] for e in range(nex)]
+    U.append(unit(4, GO, 0, hw, ("x", "z", "y"), oslots, r["o_OO"], 0))
+    U[4].go()
+
+    BQ[...] = jnp.zeros(BQ.shape, F32)
+    eight = jnp.ones((8, seq), BF)
+    XS = {}
+
+    def attend_back(k):
+        t = c.mpeer(k)[1]
+        if k:
+            H[k].wait_recv()
+
+        def head(h, _):
+            at = pl.ds(pl.multiple_of(h * HD, HD), HD)
+            g = DOT[t, at].astype(F32) * RI[t, pl.ds(h, 1)]
+            dd = jnp.sum(g * ATQ[t, at].astype(F32), axis=0, keepdims=True)
+            gl = g.astype(BF)
+            e = ET[t, h]
+            ds = (e.astype(F32) * (mm(VT[t, at], gl, 0, 0) - dd)).astype(BF)
+            dq = mm(KT[t, h, 0:HD], ds, 1, 0) * HD**-0.5
+            dk = mm(QT[t, h, 0:HD], ds, 1, 1)
+            dv = mm(gl, e, 1, 1)
+            for i, x in enumerate((dq, dk, dv)):
+                DA[t, pl.ds(pl.multiple_of(i * hw + h * HD, HD), HD), 0:seq] = x.astype(BF)
+            return 0
+
+        lax.fori_loop(0, nh, head, 0)
+        g = DA[t, 0 : 3 * hw, 0:seq]
+        BQ[:, 0 : 3 * hw] += mm(eight, g, 1, 1)
+        dx = mm(g, WT[...], 0, 0)
+        if k == 0:
+            ACC[...] += dx
+        elif k == 2:
+            XS[3].wait_recv()
+            ACT[t] = (dx + UA[0, 0:seq].astype(F32)).astype(BF)
+        else:
+            ACT[t] = dx.astype(BF)
+        if k:
+            dst = UA.at[{3: 0, 2: 1, 1: 2}[k], 0:seq]
+            XS[k] = rcopy(ACT.at[t], dst, r["xs"].at[k - 1], r["xr"].at[k - 1], yd if k == 2 else sd)
+            XS[k].start()
+
+    attend_back(0)
+    U[0].go()
+    U[1].go()
+    S.go()
+    attend_back(3)
+    U[4].go()
+    U[1].go()
+    U[0].go()
+    S.go()
+    attend_back(2)
+    U[4].go()
+    U[2].go()
+    U[3].go()
+    S.go()
+    attend_back(1)
+    S.go()
+
+    def qkv_grad(i, _):
+        at = pl.ds(pl.multiple_of(i * hw, 16), hw)
+        g = mm(DA[0, at, 0:seq], TOK[0], 1, 0)
+        for t in range(1, 4):
+            g += mm(DA[t, at, 0:seq], TOK[t], 1, 0)
+        UA[3, at] = g.astype(BF)
+        return 0
+
+    lax.fori_loop(0, 3, qkv_grad, 0)
+    n3 = 3 * hw
+    qslots = [GP.at[0:1, 0 : n3 // 2], GP.at[1:2, 0 : n3 // 4]]
+    qslots += [GP.at[2:3, e * (n3 // 4) : (e + 1) * (n3 // 4)] for e in range(min(nex, 3))]
+    qslots += [GP.at[3:4, e * (n3 // 4) : (e + 1) * (n3 // 4)] for e in range(max(nex - 3, 0))]
+    U[4].go()
+    Q = Unit(
+        c, lambda h, off, n: view(UA, 0)(3, off, n), n3, ("x", "z"), qslots, us.at[5], ur.at[5],
+        rows_of(r["o_OQ"], 0), r["os"].at[7],
+    )
+    Q.go()
+    B = Swap(BQ, r["BQR"], r["zs"], r["zr"], dps)
+    B.go()
+    L[1].wait_recv()
+    L[3].start()
+    for x in L[:3]:
+        (x.wait if x is L[0] else x.wait_send)()
+    XS[1].wait_recv()
+    XS[2].wait_recv()
+
+    def finish(i, _):
+        at = pl.ds(pl.multiple_of(i * nr, nr), nr)
+        LOB[at] = (ACC[at] + UA[1, at].astype(F32) + UA[2, at].astype(F32)).astype(BF)
+        return 0
+
+    lax.fori_loop(0, seq // nr, finish, 0)
+    T = spread(TG, 3)
+    U.append(Q)
+    live = True
+    while live:
+        live = False
+        for u in U + [S, B]:
+            n = len(u.steps) if isinstance(u, Unit) else len(u.cps)
+            if u.at <= n:
+                u.go()
+                live = True
+    r["o_OS"][...] = SG[...]
+    r["o_OB"][...] = BQ[...]
+    T[1].wait_recv()
+    T[3].start()
+    T[0].wait()
+    for x in (T[1], T[2], T[3], L[3]):
         x.wait_send()
-    outs = [n for n in names if n.startswith("o_")]
-    cps = [pltpu.make_async_copy(r[n[2:]], r[n], r["os"].at[i]) for i, n in enumerate(outs)]
-    for x in cps:
-        x.start()
-    for x in cps:
-        x.wait()
-
-
-def forward(tok4, lengths, vec, wq, wk, wv, wo, wu, wd, nbits):
+    for x in (T[2], T[3], L[2], L[3]):
+        x.wait_recv()
+    for x in V + A + C[:3] + [M] + list(H.values()) + list(XS.values()):
+        x.wait_send()
+    for u in U:
+        u.drain()
+
+
+ORDERS = (("z", "x", "y"), ("x", "y", "z"), ("z", "x", "y"), ("x", "y", "z"))
+
+
+def layer(tok4, cot4, lengths, vec, wq, wk, wv, wo, wu, wd, nbits):
     nt, seq, d = tok4.shape
     hw = wq.shape[1]
     ff = wu.shape[1]
@@ -284,6 +708,7 @@
     V = pltpu.VMEM
     S = jax.ShapeDtypeStruct
     DMA = pltpu.SemaphoreType.DMA
+    nex = nbits - 2
     scratch = {
         "TOK": V((nt, seq, d), BF),
         "W3": V((3, d, hw), BF),
@@ -297,7 +722,6 @@
         "ATO": V((nt, hw, seq), BF),
         "N1": V((seq, d), F32),
         "I1": V((seq, 1), F32),
-        "FIRST": V((seq, d), F32),
         "FL": V((seq, d), BF),
         "ACT": V((nt, seq, ff), BF),
         "GP": V((nt, seq, ff), BF),
@@ -306,44 +730,89 @@
         "DA": V((nt, ff, d), BF),
         "VA": V((nt, 8, d), F32),
         "ACC": V((seq, d), F32),
-        "N2": V((seq, d), F32),
-        "I2": V((seq, 1), F32),
-        "ls": DMA((10,)),
+        "COT": V((seq, d), BF),
+        "SA": V((2, seq, ff), BF),
+        "SH": V((2, seq, ff), BF),
+        "SFL": V((seq, d), BF),
+        "SD2": V((seq, d), BF),
+        "D2L": V((seq, d), BF),
+        "SAT": V((2, hw, seq), BF),
+        "DOT": V((nt, hw, seq), BF),
+        "DTS": V((nt, hw, seq), BF),
+        "SG": V((16, d), F32),
+        "SGR": V((nbits + 2, 16, d), F32),
+        "BQ": V((8, d), F32),
+        "BQR": V((nbits, 8, d), F32),
+        "GD": V((2, ff, d), BF),
+        "GU": V((2, d, ff), BF),
+        "GO": V((2, hw, d), BF),
+        "ls": DMA((11,)),
         "gs": DMA((3, 7)),
         "gr": DMA((3, 7)),
         "vs": DMA((3,)),
         "vr": DMA((3,)),
         "as": DMA((3,)),
         "ar": DMA((3,)),
-        "os": DMA((24,)),
+        "cs": DMA((5,)),
+        "cr": DMA((5,)),
+        "bs": DMA((4,)),
+        "br": DMA((4,)),
+        "ps": DMA((6,)),
+        "pr": DMA((6,)),
+        "us": DMA((6, 8 + nex)),
+        "ur": DMA((6, 8 + nex)),
+        "hs": DMA((3,)),
+        "hr": DMA((3,)),
+        "xs": DMA((3,)),
+        "xr": DMA((3,)),
+        "ws": DMA((nbits + 2,)),
+        "wr": DMA((nbits + 2,)),
+        "zs": DMA((nbits,)),
+        "zr": DMA((nbits,)),
+        "os": DMA((8,)),
     }
-    ins = {"len": lengths, "vec": vec, "tok": tok4, "wq": wq, "wk": wk, "wv": wv, "wo": wo, "wu": wu, "wd": wd}
-    specs = [pl.BlockSpec(memory_space=pltpu.SMEM), pl.BlockSpec(memory_space=V)]
-    specs += [pl.BlockSpec(memory_space=pl.ANY)] * (len(ins) - 2)
-    outs = [
-        "QT", "KT", "VT", "ET", "RI", "ATQ", "ATO", "N1", "I1", "FL", "ACT", "GP", "WOA", "UA", "DA", "N2", "I2",
-    ]
+    for j, (rows, order) in enumerate([(ff // 2, o) for o in ORDERS] + [(hw, ("x", "z", "y"))]):
+        n, h = rows, 2
+        for i, ax in enumerate(order):
+            if ax == "y":
+                h = 1
+            else:
+                n //= 2
+            scratch["R%d%d" % (j, i)] = V((h, n, d), BF)
+        scratch["X%d" % j] = V((max(nex, 1), 1, n, d), BF)
+    ins = {
+        "len": lengths, "vec": vec, "tok": tok4, "cot": cot4,
+        "wq": wq, "wk": wk, "wv": wv, "wo": wo, "wu": wu, "wd": wd,
+    }
+    A = pl.BlockSpec(memory_space=pl.ANY)
+    B = pl.BlockSpec(memory_space=V)
+    specs = [pl.BlockSpec(memory_space=pltpu.SMEM), B] + [A] * (len(ins) - 2)
+    outs = {
+        "LO": (S((nt, seq, d), BF), A),
+        "TG": (S((nt, seq, d), BF), A),
+        "OU": (S((d, ff), BF), A),
+        "OD": (S((ff, d), BF), A),
+        "OO": (S((hw, d), BF), A),
+        "OQ": (S((3 * hw, d), BF), A),
+        "OS": (S((16, d), F32), B),
+        "OB": (S((8, d), F32), B),
+    }
     names = list(ins) + ["o_" + n for n in outs] + list(scratch)
+
+    def kernel(*refs):
+        layer_kernel(nbits, names, *refs)
+
     res = pl.pallas_call(
-        functools.partial(fwd_kernel, nbits, names),
-        out_shape=[S(scratch[n].shape, scratch[n].dtype) for n in outs],
+        kernel,
+        out_shape=[o[0] for o in outs.values()],
         in_specs=specs,
-        out_specs=[pl.BlockSpec(memory_space=pl.ANY)] * len(outs),
+        out_specs=[o[1] for o in outs.values()],
         scratch_shapes=list(scratch.values()),
         compiler_params=pltpu.CompilerParams(
             collective_id=0, has_side_effects=True, vmem_limit_bytes=60 * 2**20
         ),
     )(*ins.values())
     return dict(zip(outs, res))
-
-
-def norm_back(up, normed, inv, gain):
-    c = up * gain
-    return inv * (
-        c
-        - jnp.mean(c, axis=-1, keepdims=True)
-        - normed * jnp.mean(c * normed, axis=-1, keepdims=True)
-    )
 
 
 def shards(
@@ -354,65 +823,21 @@
     seq = rows // n
     hw = wq.shape[1]
     m = lax.axis_index("mp")
-    nd = lax.axis_size("dp")
-    own = lambda a: lax.dynamic_slice_in_dim(a, m * seq, seq, 0)
+    nbits = lax.axis_size("dp").bit_length() - 1
     f = lambda a: a.astype(F32)
     zero = jnp.zeros((hw,), F32)
     vec = jnp.stack(
         [f(a) for a in (bo, g1, s1, bd, g2, s2, bu)] + [jnp.concatenate([f(bq), zero, f(bv), zero])]
     )
-    tok4 = tokens.reshape(n, seq, d)
-    F = forward(tok4, lengths, vec, wq, wk, wv, wo, wu, wd, nd.bit_length() - 1)
-    n1, i1, n2, i2, first_low = F["N1"], F["I1"], F["N2"], F["I2"], F["FL"]
-    att_own, act, gp = F["ATO"], F["ACT"], F["GP"]
-    out_own = (n2 * f(g2) + f(s2)).astype(BF)
-    c_own = f(own(cot))
-    d2 = norm_back(c_own, n2, i2, f(g2))
-    d2l = d2.astype(BF)
-    dg2, ds2, dbd = jnp.sum(c_own * n2, 0), jnp.sum(c_own, 0), jnp.sum(d2, 0)
-    dwd = jnp.einsum("qtf,td->qfd", act, d2l, preferred_element_type=F32)
-    dact = jnp.einsum("td,qfd->qtf", d2l, F["DA"], preferred_element_type=F32)
-    dh = (dact * f(gp)).astype(BF)
-    dbu = jnp.sum(f(dh), axis=1)
-    dwu = jnp.einsum("td,qtf->qdf", first_low, dh, preferred_element_type=F32)
-    d1 = d2 + jnp.einsum("qtf,qdf->td", dh, F["UA"], preferred_element_type=F32)
-    dg1, ds1 = jnp.sum(d1 * n1, 0), jnp.sum(d1, 0)
-    dm = norm_back(d1, n1, i1, f(g1))
-    dbo = jnp.sum(dm, 0)
-    dml = dm.astype(BF)
-    dwo = jnp.einsum("qkt,td->qkd", att_own, dml, preferred_element_type=F32)
-    datt = jnp.einsum("td,qkd->qkt", dml, F["WOA"], preferred_element_type=F32).astype(BF)
-    datt = lax.all_to_all(datt, "mp", 0, 0)
-    hs = (n, hw // HD, HD, seq)
-    doh = f(datt).reshape(hs) * F["RI"][:, : hw // HD, None, :]
-    dd = jnp.sum(doh * f(F["ATQ"]).reshape(hs), axis=2, keepdims=True)
-    dol = doh.astype(BF)
-    e = F["ET"]
-    q, k, v = F["QT"][:, :, :HD], F["KT"][:, :, :HD], F["VT"].reshape(hs)
-    es = functools.partial(jnp.einsum, preferred_element_type=F32)
-    dv = es("thkq,thdq->thdk", e, dol)
-    dp = es("thdk,thdq->thkq", v, dol)
-    ds = (f(e) * (dp - dd)).astype(BF)
-    dq = es("thkq,thdk->thdq", ds, k) * HD**-0.5
-    dk = es("thkq,thdq->thdk", ds, q)
-    dq, dk, dv = (a.reshape(n, hw, seq).astype(BF) for a in (dq, dk, dv))
-    dbq, dbv = jnp.sum(f(dq), (0, 2)), jnp.sum(f(dv), (0, 2))
-    dwq, dwk, dwv = (es("tsd,tws->dw", tok4, a) for a in (dq, dk, dv))
-    back = (es("tws,dw->tsd", dq, wq) + es("tws,dw->tsd", dk, wk) + es("tws,dw->tsd", dv, wv)).astype(BF)
-    back = jnp.sum(f(lax.all_to_all(back, "mp", 0, 0)), 0)
-    tg_own = (dm + back).astype(BF)
-    layer_out = lax.all_gather(out_own, "mp", tiled=True)
-    tokens_grad = lax.all_gather(tg_own, "mp", tiled=True)
-    low = lambda a: a.astype(BF)
-    ffn = lax.psum_scatter(jnp.stack([low(dwu), low(dwd)], 1), "mp", scatter_dimension=0)
-    dwo = lax.psum_scatter(low(dwo), "mp", scatter_dimension=0)
-    dbu = lax.psum_scatter(dbu, "mp", scatter_dimension=0)
-    dwq, dwk, dwv, dwo, ffn = lax.psum((low(dwq), low(dwk), low(dwv), dwo, ffn), "dp")
-    dbq, dbv, dbu = lax.psum((dbq, dbv, dbu), "dp")
-    dbo, dg1, ds1, dbd, dg2, ds2 = lax.psum((dbo, dg1, ds1, dbd, dg2, ds2), ("dp", "mp"))
+    o = layer(
+        tokens.reshape(n, seq, d), cot.reshape(n, seq, d), lengths, vec, wq, wk, wv, wo, wu, wd, nbits
+    )
+    q, sg, b = f(o["OQ"]), o["OS"], o["OB"][0]
+    dbu = lax.dynamic_index_in_dim(sg, 8 + m, 0, False)
     return (
-        layer_out, tokens_grad, f(dwq), dbq, f(dwk), f(dwv), dbv, f(dwo), dbo, dg1, ds1,
-        f(ffn[0]), dbu, f(ffn[1]), dbd, dg2, ds2,
+        o["LO"].reshape(rows, d), o["TG"].reshape(rows, d),
+        q[:hw].T, b[:hw], q[hw : 2 * hw].T, q[2 * hw :].T, b[2 * hw : 3 * hw],
+        f(o["OO"]), sg[0], sg[1], sg[2], f(o["OU"]), dbu, f(o["OD"]), sg[3], sg[4], sg[5],
     )
 
 

time: 591 us -> 224 us (0.38); the launches traced: 583 us -> 223 us
  waiting for transfers between devices: 258 us -> 0 us
  blocking collectives: 147 us -> 0 us
  Pallas kernels: 58 us -> 195 us
  matrix products: 41.1 us -> 0 us
  other arithmetic: 28.9 us -> 6.69 us
  between operations: 14.7 us -> 0.7 us
  local copies, waits for them, and re-layouts: 31.5 us -> 20.7 us
    pallas_call x1, Pallas kernels: 58 us -> 195 us  [layer(): pl.pallas_call(kernel, out_shape=[o[0] for o in outs.values()], in_specs=...]
    psum x1 -> x0, waiting for transfers between devices: 135 us -> none  [shards(): lax.psum((low(dwq), low(dwk), low(dwv), dwo, ffn), 'dp')]
    unnamed x6 -> x0, waiting for transfers between devices: 78.6 us -> none
    all_to_all x1 -> x0, blocking collectives: 73 us -> none  [shards(): back = jnp.sum(f(lax.all_to_all(back, 'mp', 0, 0)), 0)]
    psum x2 -> x0, blocking collectives: 63.4 us -> none  [the longest x1 41.6 us: shards(): lax.psum((dbo, dg1, ds1, dbd, dg2, ds2), ('dp', 'mp'))]
    dot_general x16 -> x0, matrix products: 41.1 us -> none  [the longest x3 6.53 us: shards(): dwq, dwk, dwv = (es('tsd,tws->dw', tok4, a) for a in (dq, dk, dv))]
    reduce_scatter x1 -> x0, waiting for transfers between devices: 25.2 us -> none  [shards(): dwo = lax.psum_scatter(low(dwo), 'mp', scatter_dimension=0)]
    all_to_all x1 -> x0, waiting for transfers between devices: 19.6 us -> none  [shards(): datt = lax.all_to_all(datt, 'mp', 0, 0)]
  transfers between devices with their start and end apart: 6 -> 0, of which waited for: 4 -> 0; matrix products, arithmetic and copies ran while one was open for 7% -> 0% of each run, Pallas kernels for 0% -> 0%
where the time goes in v3:
time: 224 us; the launch traced here: 223 us
  Pallas kernels  195 us (87%)
  local copies, waits for them, and re-layouts  20.7 us (9%)
  other arithmetic  6.69 us (3%)
    pallas_call x1, Pallas kernels, layer(): pl.pallas_call(kernel, out_shape=[o[0] for o in outs.values()], in_specs=...  195 us
    unnamed x15, local copies, waits for them, and re-layouts  11 us
    convert_element_type x6, other arithmetic, shards(): f = lambda a: a.astype(F32)  6.61 us
    another operation x9, local copies, waits for them, and re-layouts, shards(): jnp.stack([f(a) for a in (bo, g1, s1, bd, g2, s2, bu)] + [jnp.concatenate...  5.45 us

profile of v3, /device:TPU:0, one launch (start us, length us, event | category | flops | bytes accessed | tf_op | source)
XLA Modules:
  0.0 223.4 jit_solution(6328613183163571290)
XLA Ops:
  0.7 1.9 copy.35.refs_4_
  2.5 1.9 copy.36.refs_5_
  4.4 1.9 copy.37.refs_6_
  6.3 0.7 convert_element_type.12
  6.9 0.7 convert_element_type.26
  7.7 0.7 reshape.52
  8.4 0.7 reshape.53
  9.1 0.7 reshape.54
  9.8 0.7 reshape.55
  10.4 0.7 reshape.56
  11.1 0.7 reshape.57
  11.8 0.7 reshape.58
  12.5 0.6 stack.63.refs_1_
  13.1 195.4 %shard_map.305 = (bf16[4,512,768]{2,1,0:T(8,128)(2,1)}, bf16[4,512,768]{2,1,0:T(8,128)(2,1)}, bf16[768,768]{1,0:T(8,128)(2,1)}, bf16[768,768]{1,0:T(8,128)(2,1)}...) custom-call(s32[4]{0:T(128)} %refs_0_.1, ...), custom_call_target="tpu_custom_call" | custom-call | tf_op jit(solution)/shard_map/pallas_call | solution.py:805
  208.5 1.6 slice_reduce_fusion
  210.1 1.3 convert_element_type.27
  211.4 1.2 slice_bitcast_fusion
  212.7 1.4 fusion
  214.1 1.6 convert_element_type.29
  215.7 1.6 convert_element_type.30
  217.2 0.9 convert_element_type.28
  218.7 1.7 copy.40
  220.4 1.4 copy-done
  221.7 1.7 copy.41
  (12 shorter events, 0.7 us)
Async XLA Ops:
  211.4 2.6 %copy-start.3 = (bf16[768,768]{1,0:T(8,128)(2,1)S(1)}, bf16[768,768]{1,0:T(8,128)(2,1)}, u32[]{:S(2)}) copy-start(bf16[768,768]{1,0:T(8,128)(2,1)} %get-tuple-element.31) | copy-start | bytes 3538948
  212.7 3.0 %copy-start.2 = (bf16[768,768]{1,0:T(8,128)(2,1)S(1)}, bf16[768,768]{1,0:T(8,128)(2,1)}, u32[]{:S(2)}) copy-start(bf16[768,768]{1,0:T(8,128)(2,1)} %get-tuple-element.32) | copy-start | bytes 3538948
  215.7 1.6 copy-start.4
  215.7 3.1 %copy-start.1 = (bf16[4,512,768]{2,1,0:T(8,128)(2,1)S(1)}, bf16[4,512,768]{2,1,0:T(8,128)(2,1)}, u32[]{:S(2)}) copy-start(bf16[4,512,768]{2,1,0:T(8,128)(2,1)} %get-tuple-element.25) | copy-start | bytes 9437188
  218.7 3.0 %copy-start = (bf16[4,512,768]{2,1,0:T(8,128)(2,1)S(1)}, bf16[4,512,768]{2,1,0:T(8,128)(2,1)}, u32[]{:S(2)}) copy-start(bf16[4,512,768]{2,1,0:T(8,128)(2,1)} %get-tuple-element.26) | copy-start | bytes 9437188
